TPU v7x, 256 devices: a whole 4x4x8 slice. The times are simulated.
256 devices in a mesh: row: 16 (over z, core), col: 16 (over y, x).
Axes of the slice: x: 4, y: 4, z: 8, core: 2. Of those that a mesh axis runs over, the one named last changes fastest.
Arguments:
- feats: bfloat16 [32768, 256], P(('row', 'col')), may hold values from -6 to 6
- tiles: bfloat16 [256, 192, 128, 128], P(('row', 'col')), may hold values from 0.099609375 to 1
- tile_row: int32 [256, 192], P(('row', 'col')), may hold values from 0 to 15
- tile_col: int32 [256, 192], P(('row', 'col')), may hold values from 0 to 15
- counts: int32 [256], P(('row', 'col')), may hold values from 48 to 192, as said below
- w_self: bfloat16 [256, 256], replicated, may hold values from -0.375 to 0.375
- w_neigh: bfloat16 [256, 256], replicated, may hold values from -0.375 to 0.375
- bias: float32 [256], replicated, may hold values from -4 to 4
- grad_out: bfloat16 [32768, 256], P(('row', 'col')), may hold values from -6 to 6
Outputs:
- output: bfloat16 [32768, 256], P(('row', 'col'))
- d_feats: bfloat16 [32768, 256], P(('row', 'col'))
- d_wself: float32 [256, 256], replicated
- d_wneigh: float32 [256, 256], replicated
- d_bias: float32 [256], replicated
Inputs may be any that keep to these rules, and one draw needn't show every extreme that they name: `counts`: each device uses between a quarter of its 192 slots and all of them; some device uses all.
All inputs are finite; a program needn't handle non-finite values.
Results may differ from a plain program's by a relative error of at most 0.019.
Values may be sent and summed in bfloat16 or wider, within the bound.
A program may use at most 128 MiB of HBM per device.

v0:
```python
import jax
import jax.numpy as jnp
from jax import lax
from jax.sharding import PartitionSpec as P


def own_layer(node_feats, mixed_sum, degree, node_grads, w_self, w_neigh, bias):
    scaling = lax.rsqrt(1.0 + degree)[:, None]
    mixed = (mixed_sum * scaling).astype(jnp.bfloat16)
    pre = (
        jnp.dot(node_feats, w_self, preferred_element_type=jnp.float32)
        + jnp.dot(mixed, w_neigh, preferred_element_type=jnp.float32)
        + bias
    )
    sigmoid_val = jax.nn.sigmoid(pre)
    output = (pre * sigmoid_val).astype(jnp.bfloat16)
    slope = sigmoid_val * (1.0 + pre * (1.0 - sigmoid_val))
    grad_pre = (node_grads.astype(jnp.float32) * slope).astype(jnp.bfloat16)
    back_rows = (jnp.dot(grad_pre, w_neigh.T, preferred_element_type=jnp.float32) * scaling).astype(
        jnp.bfloat16
    )
    return (mixed, output, grad_pre, back_rows)


def per_device(feats, tiles, tile_row, tile_col, counts, w_self, w_neigh, bias, grad_out):
    n_rows = lax.axis_size("row")
    n_cols = lax.axis_size("col")
    node_dev = feats.shape[0]
    tile_side = tiles.shape[2]
    slot_count = tiles.shape[1]
    row_tiles = node_dev * n_cols // tile_side
    col_tiles = node_dev * n_rows // tile_side
    usable = jnp.arange(slot_count, dtype=jnp.int32) < counts[0]
    masked = jnp.where(usable[:, None, None], tiles[0], jnp.zeros((), tiles.dtype)).astype(
        jnp.float32
    )
    my_rows = tile_row[0]
    my_cols = tile_col[0]
    dense_block = jnp.zeros((row_tiles, tile_side, col_tiles, tile_side), jnp.float32)
    dense_block = dense_block.at[my_rows, :, my_cols, :].add(masked)
    dense_block = dense_block.reshape(row_tiles * tile_side, col_tiles * tile_side)
    column_block = lax.all_gather(feats, "row", axis=0, tiled=True)
    partial_value = jnp.dot(
        dense_block, column_block.astype(jnp.float32), precision=lax.Precision.HIGHEST
    )
    degree_part = jnp.sum(dense_block, axis=1)
    block_sums, block_degree = lax.psum((partial_value, degree_part), "col")
    block_feats, block_grads = (
        lax.all_gather(feats, "col", axis=0, tiled=True),
        lax.all_gather(grad_out, "col", axis=0, tiled=True),
    )
    mixed_all, output_all, grad_all, block_back = own_layer(
        block_feats, block_sums, block_degree, block_grads, w_self, w_neigh, bias
    )
    offset = lax.axis_index("col") * node_dev
    mixed = lax.dynamic_slice_in_dim(mixed_all, offset, node_dev, 0)
    output = lax.dynamic_slice_in_dim(output_all, offset, node_dev, 0)
    grad_pre = lax.dynamic_slice_in_dim(grad_all, offset, node_dev, 0)
    grad_terms = (
        jnp.dot(feats.T, grad_pre, preferred_element_type=jnp.float32),
        jnp.dot(mixed.T, grad_pre, preferred_element_type=jnp.float32),
        jnp.sum(grad_pre, axis=0, dtype=jnp.float32),
    )
    d_wself, d_wneigh, d_bias = lax.psum(
        (grad_terms[0], grad_terms[1], grad_terms[2]), ("row", "col")
    )
    self_grad = jnp.dot(grad_pre, w_self.T, preferred_element_type=jnp.float32)
    column_terms = lax.dot_general(
        dense_block,
        block_back.astype(jnp.float32),
        (((0,), (0,)), ((), ())),
        precision=lax.Precision.HIGHEST,
    )
    own_back = lax.psum_scatter(
        column_terms.astype(jnp.bfloat16), "row", scatter_dimension=0, tiled=True
    ).astype(jnp.float32)
    d_feats = (self_grad + own_back).astype(jnp.bfloat16)
    return (output, d_feats, d_wself, d_wneigh, d_bias)


def solution(mesh):
    placed = (
        P(("row", "col"), None),
        P(("row", "col"), None, None, None),
        P(("row", "col"), None),
        P(("row", "col"), None),
        P(("row", "col")),
        P(),
        P(),
        P(),
        P(("row", "col"), None),
    )
    return jax.shard_map(
        per_device,
        mesh=mesh,
        in_specs=placed,
        out_specs=(P(("row", "col"), None), P(("row", "col"), None), P(), P(), P()),
        check_vma=False,
    )
```

profile of v0, /device:TPU:1, one launch (start us, length us, event | category | flops | bytes accessed | tf_op | source)
XLA Modules:
  0.0 583.5 jit_solution(1682427682954309617)
XLA Ops:
  7.2 0.7 all-gather.6.cloned.1.call-update
  7.9 0.0 all-gather.4.cloned.1.call-start
  8.0 0.7 all-gather.4.cloned.1.call-update
  8.7 0.0 all-reduce.4.cloned.1.call-start
  9.4 0.7 or_select_fusion
  10.1 8.2 %fusion.6 = f32[192,128,128]{2,1,0:T(8,128)} fusion(bf16[1,192,128,128]{3,2,1,0:T(8,128)(2,1)} %param.10, pred[192]{0:T(512)(128)(4,1)S(1)} %iota_compare_fusion), kind=kLoop, calls=%fused_computation.8 | loop fusion | flops 6291456 | bytes 18874560 | tf_op jit(solution)/shard_map/convert_element_type | solution.py:34
  18.3 7.8 %broadcast_in_dim.20 = f32[16,128,16,128]{3,1,2,0:T(8,128)} broadcast(f32[]{:T(128)} %constant.8.clone.1), dimensions={} | broadcast | bytes 16777220 | tf_op jit(solution)/shard_map/broadcast_in_dim | solution.py:39
  26.2 41.2 %scatter_fusion = f32[16,128,16,128]{3,1,2,0:T(8,128)} fusion(f32[16,128,16,128]{3,1,2,0:T(8,128)} %broadcast_in_dim.20, s32[192]{0:T(256)S(1)} %bitcast.35, f32[192,128,128]{2,1,0:T(8,128)} %fusion.6), kind=kCustom, calls=%fused_computation | custom fusion | flops 3145728 | bytes 37750272 | tf_op jit(solution)/shard_map/scatter-add | solution.py:40
  67.3 17.7 %copy.15 = f32[16,128,16,128]{3,2,1,0:T(8,128)} copy(f32[16,128,16,128]{3,1,2,0:T(8,128)} %scatter_fusion) | data formatting | bytes 33554432 | tf_op jit(solution)/shard_map/scatter-add | solution.py:40
  85.0 18.7 %fusion.2 = f32[2048,256]{1,0:T(8,128)} fusion(bf16[2048,256]{1,0:T(8,128)(2,1)} %all-gather.6.cloned.1.call-done, f32[256,8,16,128]{3,2,1,0:T(8,128)} %bitcast.33), kind=kOutput, calls=%fused_computation.3 | convolution fusion | flops 12884901888 | bytes 19922944 | tf_op jit(solution)/shard_map/dot_general | solution.py:43
  103.7 0.0 all-gather.8.cloned.1.call-start
  103.8 0.5 all-gather.8.cloned.1.call-update
  104.3 0.3 all-reduce.6.cloned.1.call-start
  104.6 6.6 %reduce_sum.20 = f32[16,128]{1,0:T(8,128)S(1)} reduce(f32[16,128,16,128]{3,1,2,0:T(8,128)} %scatter_fusion, f32[]{:T(128)} %constant.8.clone.1), dimensions={2,3}, to_apply=%region_2.3 | reduce | flops 4192256 | bytes 16785412 | tf_op jit(solution)/shard_map/reduce_sum | solution.py:46
  111.2 35.2 %psum.36 = f32[2048]{0:T(1024)S(1)} all-reduce(f32[2048]{0:T(1024)S(1)} %bitcast.36), channel_id=1, replica_groups=mesh['row'=16,'col'=16] {'col'}, use_global_device_ids=true, to_apply=%region_3.4 | all-reduce | flops 2048 | bytes 16384 | tf_op jit(solution)/shard_map/psum | solution.py:47
  146.5 1.6 fusion.23
  148.1 59.1 %all-reduce.4.cloned.1.call-done = f32[2048,256]{1,0:T(8,128)} async-done(((f32[2048,256]{1,0:T(8,128)}), f32[2048,256]{1,0:T(8,128)}) %all-reduce.4.cloned.1.call-update) | async-done | bytes 2097168 | tf_op jit(solution)/shard_map/psum | solution.py:47
  207.2 2.9 multiply_convert_fusion.1
  210.1 46.5 %all-gather.8.cloned.1.call-done = bf16[2048,256]{1,0:T(8,128)(2,1)} async-done(((bf16[128,256]{1,0:T(8,128)(2,1)}), bf16[2048,256]{1,0:T(8,128)(2,1)}) %all-gather.8.cloned.1.call-update) | async-done | bytes 1048592 | tf_op jit(solution)/shard_map/all_gather | solution.py:50
  256.6 4.5 multiply_convert_fusion
  261.2 1.8 fusion.14
  262.9 0.9 convolution_bitcast_fusion
  263.8 0.5 fusion.8
  264.3 0.0 reduce-scatter.2.cloned.1.call-start
  264.4 22.6 %fusion.9 = bf16[2048,256]{1,0:T(8,128)(2,1)} fusion(bf16[2048,256]{1,0:T(8,128)(2,1)S(1)} %fusion.8, f32[256,8,16,128]{3,2,1,0:T(8,128)} %bitcast.34), kind=kOutput, calls=%fused_computation.13 | convolution fusion | flops 12885426176 | bytes 18874368 | tf_op jit(solution)/shard_map/dot_general | solution.py:68
  287.1 77.0 %psum.39 = f32[256]{0:T(256)} all-reduce(f32[256]{0:T(256)S(1)} %convert_reduce_fusion), channel_id=1, replica_groups=mesh['row'=16,'col'=16] {'row','col'}, use_global_device_ids=true, to_apply=%region_8.9 | all-reduce | flops 256 | bytes 2048 | tf_op jit(solution)/shard_map/psum | solution.py:64
  364.1 1.6 fusion.13
  365.7 150.5 %all-reduce.6.cloned.1.call-done = (f32[256,256]{0,1:T(8,128)}, f32[256,256]{1,0:T(8,128)}) async-done(((f32[256,256]{0,1:T(8,128)}, f32[256,256]{1,0:T(8,128)}), (f32[256,256]{0,1:T(8,128)}, f32[256,256]{1,0:T(8,128)})) %all-reduce.6.cloned.1.call-update) | async-done | bytes 524304 | tf_op jit(solution)/shard_map/psum | solution.py:64
  516.2 1.8 copy.16
  518.0 55.3 %reduce-scatter.2.cloned.1.call-done = bf16[128,256]{1,0:T(8,128)(2,1)} async-done(((bf16[2048,256]{1,0:T(8,128)(2,1)}), bf16[128,256]{1,0:T(8,128)(2,1)}) %reduce-scatter.2.cloned.1.call-update) | async-done | bytes 65552 | tf_op jit(solution)/shard_map/reduce_scatter | solution.py:74
  573.3 1.7 fusion.12
  575.0 1.7 copy.33
  (17 shorter events, 0.2 us)
Async XLA Ops:
  7.2 249.5 %copy-start = (bf16[256,256]{1,0:T(8,128)(2,1)S(1)}, bf16[256,256]{1,0:T(8,128)(2,1)}, u32[]{:S(2)}) copy-start(bf16[256,256]{1,0:T(8,128)(2,1)} %param.15) | copy-start | bytes 393220
  7.2 77.9 %all-gather.6.cloned.1.call-start = ((), (), s32[]{:S(2)}) async-start(), calls=%async_computation.2 | async-start | bytes 1114112 | tf_op jit(solution)/shard_map/all_gather | solution.py:42
  7.9 138.5 %all-gather.4.cloned.1.call-start = ((), (), s32[]{:S(2)}) async-start(), calls=%async_computation.1 | async-start | bytes 1114112 | tf_op jit(solution)/shard_map/all_gather | solution.py:49
  8.7 198.5 %all-reduce.4.cloned.1.call-start = ((), (), s32[]{:S(2)}) async-start(), calls=%async_computation.3 | async-start | bytes 4194304 | tf_op jit(solution)/shard_map/psum | solution.py:47
  103.7 152.9 %all-gather.8.cloned.1.call-start = ((), (), s32[]{:S(2)}) async-start(), calls=%async_computation.4 | async-start | bytes 1114112 | tf_op jit(solution)/shard_map/all_gather | solution.py:50
  104.3 42.2 %copy-start.2 = (bf16[256,256]{1,0:T(8,128)(2,1)S(1)}, bf16[256,256]{1,0:T(8,128)(2,1)}, u32[]{:S(2)}) copy-start(bf16[256,256]{1,0:T(8,128)(2,1)} %param.14) | copy-start | bytes 393220
  104.3 411.9 %all-reduce.6.cloned.1.call-start = ((), (), s32[]{:S(2)}) async-start(), calls=%async_computation.6 | async-start | bytes 1048576 | tf_op jit(solution)/shard_map/psum | solution.py:64
  148.1 108.5 %copy-start.3 = (f32[256]{0:T(256)S(1)}, f32[256]{0:T(256)}, u32[]{:S(2)}) copy-start(f32[256]{0:T(256)} %param.16) | copy-start | bytes 3076
  210.1 52.8 %copy-start.1 = (bf16[128,256]{1,0:T(8,128)(2,1)S(1)}, bf16[128,256]{1,0:T(8,128)(2,1)}, u32[]{:S(2)}) copy-start(bf16[128,256]{1,0:T(8,128)(2,1)} %param.9) | copy-start | bytes 196612
  264.3 309.0 %reduce-scatter.2.cloned.1.call-start = ((), (), s32[]{:S(2)}) async-start(), calls=%async_computation.5 | async-start | bytes 1114112 | tf_op jit(solution)/shard_map/reduce_scatter | solution.py:74
Sparse Core Ops, SparseCore 0:
  9.8 42.7 all-gather.5
  55.1 44.5 all-gather.3
  103.8 103.2 all-reduce.3
  209.8 46.8 all-gather.7
  264.5 251.7 all-reduce.5
  518.7 54.5 reduce-scatter.1
where the time goes:
time: 587 us; the launch traced here: 583 us
  waiting for transfers between devices  313 us (53%)
  blocking collectives  112 us (19%)
  other arithmetic  61.3 us (10%)
  matrix products  52.3 us (9%)
  local copies, waits for them, and re-layouts  29 us (5%)
  between operations  14.8 us (3%)
    psum x1, waiting for transfers between devices, per_device(): lax.psum((grad_terms[0], grad_terms[1], grad_terms[2]), ('row', 'col'))  150 us
    psum x1, blocking collectives, per_device(): lax.psum((grad_terms[0], grad_terms[1], grad_terms[2]), ('row', 'col'))  77 us
    psum x1, waiting for transfers between devices, per_device(): block_sums, block_degree = lax.psum((partial_value, degree_part), 'col')  59.1 us
    reduce_scatter x1, waiting for transfers between devices, per_device(): lax.psum_scatter(column_terms.astype(jnp.bfloat16), 'row', scatter_dimens...  55.3 us
    all_gather x1, waiting for transfers between devices, per_device(): lax.all_gather(grad_out, 'col', axis=0, tiled=True)  46.5 us
    scatter-add x1, other arithmetic, per_device(): dense_block = dense_block.at[my_rows, :, my_cols, :].add(masked)  41.2 us
    psum x1, blocking collectives, per_device(): block_sums, block_degree = lax.psum((partial_value, degree_part), 'col')  35.2 us
    dot_general x1, matrix products, per_device(): lax.dot_general(dense_block, block_back.astype(jnp.float32), (((0,), (0,)...  22.6 us
  transfers between devices with their start and end apart: 6, of which 4 were waited for; matrix products, arithmetic and copies ran while one was open for 23% of the time, Pallas kernels for 0%

commit v1 on v0

v1 whole, which is shorter than its diff:
```python
import jax
import jax.numpy as jnp
from jax import lax
from jax.experimental import pallas as pl
from jax.experimental.pallas import tpu as pltpu
from jax.sharding import PartitionSpec as P

MESH = pl.DeviceIdType.MESH
F32 = jnp.float32
BF16 = jnp.bfloat16
NZ, NY, NX = 8, 4, 4
NC = NY * NX
NR = 2 * NZ
T = 128
F = 256
SLOTS = 192
TILE_CUTS = 6
CUT = SLOTS // TILE_CUTS
PART = F // NZ
WPART = PART + 16
NT = (((1,), (1,)), ((), ()))
TN = (((0,), (0,)), ((), ()))


def layer_kernel(
    feats, tiles, tile_row, tile_col, counts, w_self, w_neigh, bias, grad_out,
    out, d_feats, d_wself, d_wneigh, d_bias,
    tiles_v, run, tab_v, tab, a_ref, at_ref, acc, x_all, part, part_in, degs, deg_in, pre_self, own_sum,
    back_all, sib_out, sib_in, comb, comb_in, grads, grads_in, w1_out, w1_in, w2_in, w3, w3_in, self_grad,
    tile_sem, tab_sem, agz_s, agz_r, sib_s, sib_r, deg_s, deg_r, rs_s, rs_r, ag_s, ag_r, bs_s, bs_r, rz_s, rz_r,
    w0_s, w0_r, w1_s, w1_r, w2_s, w2_r, w3_s, w3_r, w4_s, w4_r,
):
    row = lax.axis_index("row")
    col = lax.axis_index("col")
    z, k = row // 2, row % 2
    y, x = col // NX, col % NX
    sibling = (z * 2 + (1 - k), col)

    def z_to(d):
        return (((z + d) % NZ) * 2 + k, col)

    def xy_index(p):
        return ((y + p // NX) % NY) * NX + (x + p % NX) % NX

    def xy_from(p):
        return ((y + NY - p // NX) % NY) * NX + (x + NX - p % NX) % NX

    def loop(lower, upper, body):
        def step(i, carry):
            body(i)
            return carry

        lax.fori_loop(lower, upper, step, 0)

    def remote(src, dst, send, recv, where):
        return pltpu.make_async_remote_copy(
            src_ref=src, dst_ref=dst, send_sem=send, recv_sem=recv, device_id=where, device_id_type=MESH
        )

    def tile_copy(i):
        cut = pl.ds(i * CUT, CUT)
        return pltpu.make_async_copy(tiles.at[cut], tiles_v.at[cut], tile_sem.at[i])

    for i in range(TILE_CUTS):
        tile_copy(i).start()

    barrier = pltpu.get_barrier_semaphore()
    pl.semaphore_signal(barrier, inc=1, device_id=sibling, device_id_type=MESH)
    loop(1, NZ, lambda d: pl.semaphore_signal(barrier, inc=1, device_id=z_to(d), device_id_type=MESH))
    loop(1, NC, lambda p: pl.semaphore_signal(barrier, inc=1, device_id=(row, xy_index(p)), device_id_type=MESH))

    key_row = tile_row[...] * NR + tile_col[...]
    lane = lax.broadcasted_iota(jnp.int32, (1, SLOTS), 1)
    key_row = jnp.where(lane < counts[0], key_row, 4096)
    first = lax.broadcasted_iota(jnp.int32, (SLOTS, SLOTS), 0)
    second = lax.broadcasted_iota(jnp.int32, (SLOTS, SLOTS), 1)
    keys = jnp.broadcast_to(key_row, (SLOTS, SLOTS))
    key_col = jnp.sum(jnp.where(first == second, keys, 0), axis=1, keepdims=True)
    before = jnp.max(jnp.where((key_col == keys) & (first < second), first, -1), axis=0, keepdims=True)
    place = lax.broadcasted_iota(jnp.int32, (SLOTS, F), 1)
    slot = lax.broadcasted_iota(jnp.int32, (SLOTS, F), 0)
    last = jnp.max(jnp.where(key_col == place, slot, -1), axis=0, keepdims=True)
    tab_v[0:1, 0:SLOTS] = jnp.where(before < 0, SLOTS, before)
    tab_v[1:2, :] = jnp.where(last < 0, SLOTS, last)
    tab_copy = pltpu.make_async_copy(tab_v, tab, tab_sem)
    tab_copy.start()
    x_all[row] = feats[...]
    run[SLOTS] = jnp.zeros((T, T), F32)
    pl.semaphore_wait(barrier, 1 + (NZ - 1) + (NC - 1))

    def agz(d):
        return remote(feats, x_all.at[row], agz_s.at[d], agz_r.at[d], z_to(d))

    def near_first(i):
        return jnp.where(i % 2 == 1, (i + 1) // 2, NZ - i // 2)

    loop(1, NZ, lambda i: agz(NZ - near_first(i)).start())

    def to_sibling(zp):
        return remote(x_all.at[zp * 2 + k], x_all.at[zp * 2 + k], sib_s.at[zp], sib_r.at[zp], sibling)

    to_sibling(z).start()

    tab_copy.wait()
    for i in range(TILE_CUTS):
        tile_copy(i).wait()

        def add_up(s):
            run[s] = run[tab[0, s]] + tiles_v[s].astype(F32)

        loop(i * CUT, (i + 1) * CUT, add_up)

    def assemble(c):
        rows = pl.ds(pl.multiple_of(c * T, T), T)
        total = jnp.zeros((T, T), F32)
        for r in range(NR):
            block = run[tab[1, c * NR + r]]
            total = total + block
            a_ref[r // 2, rows, (r % 2) * T : (r % 2 + 1) * T] = block.astype(BF16)
        degs[c] = lax.dot_general(
            jnp.ones((8, T), F32), total, NT, preferred_element_type=F32, precision=lax.Precision.HIGHEST
        )

    loop(0, NC, assemble)

    def send_degree(p):
        return remote(degs.at[xy_index(p)], deg_in.at[p], deg_s.at[p], deg_r.at[p], (row, xy_index(p)))

    loop(1, NC, lambda p: send_degree(p).start())

    def multiply(matrix, index, right, add):
        def chunk(m):
            rows = pl.ds(pl.multiple_of(m * 512, 512), 512)
            term = jnp.dot(matrix[index, rows, :], right, preferred_element_type=F32)
            acc[rows, :] = acc[rows, :] + term if add else term

        loop(0, 4, chunk)

    def pair_of(ref, i):
        return jnp.concatenate([ref[2 * i], ref[2 * i + 1]], axis=0)

    to_sibling(z).wait_recv()
    multiply(a_ref, z, pair_of(x_all, z), False)

    def arrive(i):
        d = near_first(i)
        agz(d).wait_recv()
        to_sibling((z + NZ - d) % NZ).start()

    arrive(1)

    def forward(i):
        arrive(i + 1)
        zp = (z + NZ - near_first(i)) % NZ
        to_sibling(zp).wait_recv()
        multiply(a_ref, zp, pair_of(x_all, zp), True)

    loop(1, NZ - 1, forward)
    z_last = (z + NZ - NZ // 2) % NZ
    to_sibling(z_last).wait_recv()

    def send_part(p):
        return remote(part.at[xy_index(p)], part_in.at[p], rs_s.at[p], rs_r.at[p], (row, xy_index(p)))

    x_last = pair_of(x_all, z_last)

    def finish(p):
        c = xy_index(p)
        rows = pl.ds(pl.multiple_of(c * T, T), T)
        return acc[rows, :] + jnp.dot(a_ref[z_last, rows, :], x_last, preferred_element_type=F32)

    def finish_send(i):
        p = (i + 9) % (NC - 1) + 1
        part[xy_index(p)] = finish(p).astype(BF16)
        send_part(p).start()

    loop(0, NC - 1, finish_send)
    own_sum[...] = finish(0)

    def turn(q):
        for e in range(2):
            rows = pl.ds(pl.multiple_of((2 * q + e) * T, T), T)
            for r in range(NR):
                at_ref[q, r * T : (r + 1) * T, e * T : (e + 1) * T] = a_ref[
                    r // 2, rows, (r % 2) * T : (r % 2 + 1) * T
                ].T

    loop(0, NC // 2, turn)
    pre_self[...] = jnp.dot(feats[...], w_self[...], preferred_element_type=F32) + bias[...]

    own_degree = degs[col]
    for p in range(1, NC):
        send_degree(p).wait_recv()
        own_degree = own_degree + deg_in[p]
    scale_row = lax.rsqrt(1.0 + own_degree[0:1, :])
    scale = jnp.broadcast_to(scale_row, (T, T)).T
    scale = jnp.concatenate([scale, scale], axis=1)

    def take_part(i):
        p = (i + 9) % (NC - 1) + 1
        send_part(p).wait_recv()
        own_sum[...] = own_sum[...] + part_in[p].astype(F32)

    loop(0, NC - 1, take_part)

    mixed = (own_sum[...] * scale).astype(BF16)
    pre = pre_self[...] + jnp.dot(mixed, w_neigh[...], preferred_element_type=F32)
    sig = 1.0 / (1.0 + jnp.exp(-pre))
    slope = sig * (1.0 + pre * (1.0 - sig))
    grad_pre = (grad_out[...].astype(F32) * slope).astype(BF16)
    back = lax.dot_general(grad_pre, w_neigh[...], NT, preferred_element_type=F32) * scale
    back_all[col] = back.astype(BF16)

    def send_back(p):
        return remote(back_all.at[col], back_all.at[col], ag_s.at[p], ag_r.at[p], (row, xy_index(p)))

    loop(0, NC - 1, lambda i: send_back((i + 9) % (NC - 1) + 1).start())
    out[...] = (pre * sig).astype(BF16)

    bias_sum = jnp.sum(grad_pre.astype(F32), axis=0, keepdims=True)
    grads[0, 0:F, :] = lax.dot_general(feats[...], grad_pre, TN, preferred_element_type=F32)
    grads[1, 0:F, :] = lax.dot_general(mixed, grad_pre, TN, preferred_element_type=F32)
    grads[0, F : F + 8, :] = jnp.broadcast_to(bias_sum, (8, F))
    grads[1, F : F + 8, :] = jnp.broadcast_to(bias_sum, (8, F))
    w0 = remote(grads.at[1 - k], grads_in, w0_s, w0_r, sibling)
    w0.start()
    self_grad[...] = lax.dot_general(grad_pre, w_self[...], NT, preferred_element_type=F32)
    w0.wait_recv()
    bias_two = (grads[k, F : F + 8, :] + grads_in[F : F + 8, :])[0:1, :]

    def send_w1(d):
        zp = (z + d) % NZ
        return remote(w1_out.at[zp], w1_in.at[z], w1_s.at[d], w1_r.at[d], z_to(d))

    for zp in range(NZ):
        rows = slice(zp * PART, (zp + 1) * PART)
        w1_out[zp, 0:PART, :] = (grads[k, rows, :] + grads_in[rows, :]).astype(BF16)
        w1_out[zp, PART:WPART, :] = jnp.broadcast_to(bias_two, (16, F)).astype(BF16)
    loop(1, NZ, lambda d: send_w1(d).start())
    w1_in[z] = w1_out[z]

    def await_pair(q):
        yp = (y + q // 2) % NY
        for e in range(2):
            xp = ((x // 2 + q % 2) % 2) * 2 + e
            send_back(((y + NY - yp) % NY) * NX + (x + NX - xp) % NX).wait_recv()
        return yp * 2 + (x // 2 + q % 2) % 2

    send_back((NX + x - (x + 1 - 2 * (x % 2))) % NX).wait_recv()
    multiply(at_ref, col // 2, pair_of(back_all, col // 2), False)

    def backward(q):
        index = await_pair(q)
        multiply(at_ref, index, pair_of(back_all, index), True)

    loop(1, 6, backward)

    def send_w2(p):
        return remote(w2_in.at[col], w2_in.at[col], w2_s.at[p], w2_r.at[p], (row, xy_index(p)))

    loop(1, NZ, lambda d: send_w1(d).wait_recv())
    w1_sum = w1_in[0].astype(F32)
    for zp in range(1, NZ):
        w1_sum = w1_sum + w1_in[zp].astype(F32)
    w2_in[col] = w1_sum.astype(BF16)
    loop(1, NC, lambda p: send_w2(p).start())

    backward(6)
    b_index = await_pair(7)
    b_last = pair_of(back_all, b_index)

    def finish_back(r):
        rows = pl.ds(pl.multiple_of(r * T, T), T)
        return acc[rows, :] + jnp.dot(at_ref[b_index, rows, :], b_last, preferred_element_type=F32)

    def far_first(i):
        return near_first(NZ - 1 - i)

    def to_sibling_back(zp):
        return remote(sib_out.at[zp], sib_in.at[zp], bs_s.at[zp], bs_r.at[zp], sibling)

    def give_sibling(i):
        zp = (z + far_first(i)) % NZ
        sib_out[zp] = finish_back(zp * 2 + 1 - k).astype(BF16)
        to_sibling_back(zp).start()

    loop(0, NZ, give_sibling)

    def send_comb(d):
        zp = (z + d) % NZ
        return remote(comb.at[zp], comb_in.at[d], rz_s.at[d], rz_r.at[d], z_to(d))

    def combine(zp):
        to_sibling_back(zp).wait_recv()
        return finish_back(zp * 2 + k) + sib_in[zp].astype(F32)

    def combine_send(i):
        d = far_first(i)
        zp = (z + d) % NZ
        comb[zp] = combine(zp).astype(BF16)
        send_comb(d).start()

    loop(0, NZ - 1, combine_send)
    own_sum[...] = combine(z) + self_grad[...]

    loop(1, NC, lambda p: send_w2(p).wait_recv())
    w2_sum = w2_in[0].astype(F32)
    for c in range(1, NC):
        w2_sum = w2_sum + w2_in[c].astype(F32)
    d_bias[...] = w2_sum[PART : PART + 1, :]
    w3[z] = w2_sum[0:PART, :].astype(BF16)

    def send_w3(d):
        return remote(w3.at[z], w3.at[z], w3_s.at[d], w3_r.at[d], z_to(d))

    loop(1, NZ, lambda d: send_w3(d).start())

    def take_comb(i):
        d = far_first(i)
        send_comb(d).wait_recv()
        own_sum[...] = own_sum[...] + comb_in[d].astype(F32)

    loop(0, NZ - 1, take_comb)
    d_feats[...] = own_sum[...].astype(BF16)

    loop(1, NZ, lambda d: send_w3(d).wait_recv())
    w4 = remote(w3, w3_in, w4_s, w4_r, sibling)
    w4.start()
    w4.wait_recv()
    core = jnp.full((F, F), k, jnp.int32)
    mine = w3[...].reshape(F, F).astype(F32)
    other = w3_in[...].reshape(F, F).astype(F32)
    d_wself[...] = jnp.where(core == 0, mine, other)
    d_wneigh[...] = jnp.where(core == 0, other, mine)

    def sent_z(d):
        agz(d).wait_send()
        send_w1(d).wait_send()
        send_comb(d).wait_send()
        send_w3(d).wait_send()

    loop(1, NZ, sent_z)

    def sent_xy(p):
        send_degree(p).wait_send()
        send_part(p).wait_send()
        send_back(p).wait_send()
        send_w2(p).wait_send()

    loop(1, NC, sent_xy)

    def sent_sibling(zp):
        to_sibling(zp).wait_send()
        to_sibling_back(zp).wait_send()

    loop(0, NZ, sent_sibling)
    w0.wait_send()
    w4.wait_send()


def per_device(feats, tiles, tile_row, tile_col, counts, w_self, w_neigh, bias, grad_out):
    vmem = pl.BlockSpec(memory_space=pltpu.VMEM)
    dma = pltpu.SemaphoreType.DMA
    outs = pl.pallas_call(
        layer_kernel,
        out_shape=(
            jax.ShapeDtypeStruct((T, F), BF16),
            jax.ShapeDtypeStruct((T, F), BF16),
            jax.ShapeDtypeStruct((F, F), F32),
            jax.ShapeDtypeStruct((F, F), F32),
            jax.ShapeDtypeStruct((1, F), F32),
        ),
        in_specs=[
            vmem,
            pl.BlockSpec(memory_space=pl.ANY),
            vmem,
            vmem,
            pl.BlockSpec(memory_space=pltpu.SMEM),
            vmem,
            vmem,
            vmem,
            vmem,
        ],
        out_specs=(vmem,) * 5,
        scratch_shapes=[
            pltpu.VMEM((SLOTS, T, T), BF16),
            pltpu.VMEM((SLOTS + 1, T, T), F32),
            pltpu.VMEM((8, F), jnp.int32),
            pltpu.SMEM((8, F), jnp.int32),
            pltpu.VMEM((NZ, NC * T, 2 * T), BF16),
            pltpu.VMEM((NC // 2, NR * T, 2 * T), BF16),
            pltpu.VMEM((NC * T, F), F32),
            pltpu.VMEM((NR, T, F), BF16),
            pltpu.VMEM((NC, T, F), BF16),
            pltpu.VMEM((NC, T, F), BF16),
            pltpu.VMEM((NC, 8, T), F32),
            pltpu.VMEM((NC, 8, T), F32),
            pltpu.VMEM((T, F), F32),
            pltpu.VMEM((T, F), F32),
            pltpu.VMEM((NC, T, F), BF16),
            pltpu.VMEM((NZ, T, F), BF16),
            pltpu.VMEM((NZ, T, F), BF16),
            pltpu.VMEM((NZ, T, F), BF16),
            pltpu.VMEM((NZ, T, F), BF16),
            pltpu.VMEM((2, F + 8, F), F32),
            pltpu.VMEM((F + 8, F), F32),
            pltpu.VMEM((NZ, WPART, F), BF16),
            pltpu.VMEM((NZ, WPART, F), BF16),
            pltpu.VMEM((NC, WPART, F), BF16),
            pltpu.VMEM((NZ, PART, F), BF16),
            pltpu.VMEM((NZ, PART, F), BF16),
            pltpu.VMEM((T, F), F32),
            dma((TILE_CUTS,)),
            dma,
        ]
        + [dma((NZ,))] * 4
        + [dma((NC,))] * 6
        + [dma((NZ,))] * 4
        + [dma, dma]
        + [dma((NZ,))] * 2
        + [dma((NC,))] * 2
        + [dma((NZ,))] * 2
        + [dma, dma],
        compiler_params=pltpu.CompilerParams(
            collective_id=0, has_side_effects=True, vmem_limit_bytes=56 * 2**20
        ),
        name="sage_layer",
    )(
        feats,
        tiles.reshape(SLOTS, T, T),
        tile_row,
        tile_col,
        counts,
        w_self,
        w_neigh,
        bias.reshape(1, F),
        grad_out,
    )
    return (outs[0], outs[1], outs[2], outs[3], outs[4].reshape(F))


def solution(mesh):
    placed = (
        P(("row", "col"), None),
        P(("row", "col"), None, None, None),
        P(("row", "col"), None),
        P(("row", "col"), None),
        P(("row", "col")),
        P(),
        P(),
        P(),
        P(("row", "col"), None),
    )
    return jax.shard_map(
        per_device,
        mesh=mesh,
        in_specs=placed,
        out_specs=(P(("row", "col"), None), P(("row", "col"), None), P(), P(), P()),
        check_vma=False,
    )
```

time: 587 us -> 95.7 us (0.16)
  waiting for transfers between devices: 313 us -> 0 us
  blocking collectives: 112 us -> 0 us
  Pallas kernels: 0 us -> 86.6 us
  other arithmetic: 61.3 us -> 0 us
  matrix products: 52.3 us -> 0 us
  local copies, waits for them, and re-layouts: 29 us -> 7.5 us
  between operations: 14.8 us -> 1.29 us
    psum x2 -> x0, waiting for transfers between devices: 210 us -> none  [the longest x1 150 us: per_device(): lax.psum((grad_terms[0], grad_terms[1], grad_terms[2]), ('row', 'col'))]
    psum x2 -> x0, blocking collectives: 112 us -> none  [the longest x1 77 us: per_device(): lax.psum((grad_terms[0], grad_terms[1], grad_terms[2]), ('row', 'col'))]
    pallas_call x0 -> x1, Pallas kernels: none -> 86.6 us  [per_device(): pl.pallas_call(layer_kernel, out_shape=(jax.ShapeDtypeStruct((T, F), BF16...]
    reduce_scatter x1 -> x0, waiting for transfers between devices: 55.3 us -> none  [per_device(): lax.psum_scatter(column_terms.astype(jnp.bfloat16), 'row', scatter_dimens...]
    dot_general x8 -> x0, matrix products: 52.3 us -> none  [the longest x1 22.6 us: per_device(): lax.dot_general(dense_block, block_back.astype(jnp.float32), (((0,), (0,)...]
    all_gather x3 -> x0, waiting for transfers between devices: 46.5 us -> none  [the longest x1 46.5 us: per_device(): lax.all_gather(grad_out, 'col', axis=0, tiled=True)]
    scatter-add x1 -> x0, other arithmetic: 41.2 us -> none  [per_device(): dense_block = dense_block.at[my_rows, :, my_cols, :].add(masked)]
    scatter-add x1 -> x0, local copies, waits for them, and re-layouts: 17.7 us -> none  [per_device(): dense_block = dense_block.at[my_rows, :, my_cols, :].add(masked)]
  transfers between devices with their start and end apart: 6 -> 0, of which waited for: 4 -> 0; matrix products, arithmetic and copies ran while one was open for 23% -> 0% of each run, Pallas kernels for 0% -> 0%
where the time goes in v1:
time: 95.7 us; the launch traced here: 95.4 us
  Pallas kernels  86.6 us (90%)
  local copies, waits for them, and re-layouts  7.5 us (8%)
  between operations  1.29 us (1%)
    pallas_call x1, Pallas kernels, per_device(): pl.pallas_call(layer_kernel, out_shape=(jax.ShapeDtypeStruct((T, F), BF16...  86.6 us
    unnamed x5, local copies, waits for them, and re-layouts  7.5 us

profile of v1, /device:TPU:1, one launch (start us, length us, event | category | flops | bytes accessed | tf_op | source)
XLA Modules:
  0.0 95.4 jit_solution(7404520885852510225)
XLA Ops:
  1.3 86.6 %sage_layer.1 = (bf16[128,256]{1,0:T(8,128)(2,1)}, bf16[128,256]{1,0:T(8,128)(2,1)}, f32[256,256]{1,0:T(8,128)}, f32[256,256]{1,0:T(8,128)}, f32[1,256]{1,0:T(1,128)}) custom-call(bf16[128,256]{1,0:T(8,128)(2,1)} %feats.1, bf16[192,128,128]{2,1,0:T(8,128)(2,1)} %bitcast.3, s32[1,192]{1,0:T(1,128)} %tile_row.1, s32[1,192]{1,0:T(1,128)} %tile_col.1, ...), custom_call_target="tpu_custom_call" | custom-call | tf_op jit(solution)/shard_map/sage_layer/pallas_call | solution.py:364
  87.9 1.5 %copy.20 = bf16[128,256]{1,0:T(8,128)(2,1)} copy(bf16[128,256]{1,0:T(8,128)(2,1)} %get-tuple-element.20) | data formatting | bytes 131072
  89.4 1.5 %copy.21 = bf16[128,256]{1,0:T(8,128)(2,1)} copy(bf16[128,256]{1,0:T(8,128)(2,1)} %get-tuple-element.21) | data formatting | bytes 131072
  90.8 1.7 %copy.22 = f32[256,256]{1,0:T(8,128)} copy(f32[256,256]{1,0:T(8,128)} %get-tuple-element.22) | data formatting | bytes 524288
  92.5 1.7 %copy.23 = f32[256,256]{1,0:T(8,128)} copy(f32[256,256]{1,0:T(8,128)} %get-tuple-element.23) | data formatting | bytes 524288
  94.2 1.2 %copy.24 = f32[256]{0:T(256)} copy(f32[256]{0:T(256)} %bitcast.4) | data formatting | bytes 2048

commit v2 on v1

--- a/solution.py
+++ b/solution.py
@@ -17,17 +17,53 @@
 TILE_CUTS = 6
 CUT = SLOTS // TILE_CUTS
 PART = F // NZ
+HALF = T // 2
 WPART = PART + 16
 NT = (((1,), (1,)), ((), ()))
 TN = (((0,), (0,)), ((), ()))
 
 
+def first_legs():
+    legs = []
+    for du, dv in ((2, 2), (1, 1), (3, 3), (2, 1), (1, 2), (3, 1), (1, 3), (2, 3), (3, 2), (0, 2), (1, 0), (3, 0)):
+        if (du + dv) % 2 == 0:
+            relay, along, across = (0, dv), dv, du
+        else:
+            relay, along, across = (du, 0), du, dv
+        line = across // 2 if across % 2 == 0 else 2 + across // 2
+        legs.append((du, dv, *relay, line * 4 + (4 - along) % 4))
+    return tuple(legs)
+
+
+FIRST_LEG = first_legs()
+LINES = ((2, 0), (0, 1), (0, 3))
+OWN_WAYS = ((1, 0), (2, 0), (3, 0), (0, 1), (0, 2), (0, 3))
+PAIRS = (
+    ((0, 0), (2, 0)),
+    ((0, 1), (0, 3)),
+    ((1, 0), (3, 0)),
+    ((0, 2), (2, 2)),
+    ((1, 1), (3, 1)),
+    ((1, 3), (3, 3)),
+    ((2, 1), (2, 3)),
+    ((1, 2), (3, 2)),
+)
+Z_ORDER = (4, 3, 5, 1, 7, 2, 6, 0)
+
+
+def pick(i, values):
+    chosen = values[0]
+    for n, value in enumerate(values[1:], 1):
+        chosen = jnp.where(i == n, value, chosen)
+    return chosen
+
+
 def layer_kernel(
     feats, tiles, tile_row, tile_col, counts, w_self, w_neigh, bias, grad_out,
     out, d_feats, d_wself, d_wneigh, d_bias,
-    tiles_v, run, tab_v, tab, a_ref, at_ref, acc, x_all, part, part_in, degs, deg_in, pre_self, own_sum,
-    back_all, sib_out, sib_in, comb, comb_in, grads, grads_in, w1_out, w1_in, w2_in, w3, w3_in, self_grad,
-    tile_sem, tab_sem, agz_s, agz_r, sib_s, sib_r, deg_s, deg_r, rs_s, rs_r, ag_s, ag_r, bs_s, bs_r, rz_s, rz_r,
+    tiles_v, run, tab_v, tab, a_ref, at_ref, acc, x_all, part, part_in, line_sum, line_in, degs, deg_in, pre_self, own_sum,
+    back_all, sib_out, sib_in, comb, far_in, half_in, comb_in, grads, grads_in, w1_out, w1_in, w2_in, w3, w3_in, self_grad,
+    tile_sem, tab_sem, agz_s, agz_r, sib_s, sib_r, deg_s, deg_r, rs_s, rs_r, rl_s, rl_r, ag_s, ag_r, bs_s, bs_r, rz_s, rz_r,
     w0_s, w0_r, w1_s, w1_r, w2_s, w2_r, w3_s, w3_r, w4_s, w4_r,
 ):
     row = lax.axis_index("row")
@@ -42,8 +78,11 @@
     def xy_index(p):
         return ((y + p // NX) % NY) * NX + (x + p % NX) % NX
 
-    def xy_from(p):
-        return ((y + NY - p // NX) % NY) * NX + (x + NX - p % NX) % NX
+    odd = (x + y) % 2
+
+    def at(du, dv):
+        yp = (y + (1 - odd) * du + odd * dv) % NY
+        return yp * NX + (x + odd * du + (1 - odd) * dv) % NX
 
     def loop(lower, upper, body):
         def step(i, carry):
@@ -88,13 +127,25 @@
     run[SLOTS] = jnp.zeros((T, T), F32)
     pl.semaphore_wait(barrier, 1 + (NZ - 1) + (NC - 1))
 
-    def agz(d):
-        return remote(feats, x_all.at[row], agz_s.at[d], agz_r.at[d], z_to(d))
-
-    def near_first(i):
-        return jnp.where(i % 2 == 1, (i + 1) // 2, NZ - i // 2)
-
-    loop(1, NZ, lambda i: agz(NZ - near_first(i)).start())
+    def near(side, hops):
+        sign = 1 - 2 * side
+        return remote(
+            feats, x_all.at[row], agz_s.at[2 * hops + side - 2], agz_r.at[2 * hops + side - 2], z_to(NZ + sign * hops)
+        )
+
+    def passed(side):
+        sign = 1 - 2 * side
+        block = x_all.at[((z + NZ - 2 * sign) % NZ) * 2 + k]
+        return remote(block, block, agz_s.at[4 + side], agz_r.at[4 + side], z_to(NZ + sign))
+
+    def passed_half(side):
+        sign = 1 - 2 * side
+        block = x_all.at[((z + NZ - 2 * sign) % NZ) * 2 + k, pl.ds(side * HALF, HALF)]
+        return remote(block, block, agz_s.at[6 + side], agz_r.at[6 + side], z_to(NZ + 2 * sign))
+
+    for hops in (2, 1):
+        for side in range(2):
+            near(side, hops).start()
 
     def to_sibling(zp):
         return remote(x_all.at[zp * 2 + k], x_all.at[zp * 2 + k], sib_s.at[zp], sib_r.at[zp], sibling)
@@ -121,71 +172,105 @@
             jnp.ones((8, T), F32), total, NT, preferred_element_type=F32, precision=lax.Precision.HIGHEST
         )
 
-    loop(0, NC, assemble)
+    loop(0, NC // 2, assemble)
+    for side in range(2):
+        sign = 1 - 2 * side
+        near(side, 2).wait_recv()
+        passed_half(side).start()
+        passed(side).start()
+        to_sibling((z + NZ - 2 * sign) % NZ).start()
+    loop(NC // 2, NC, assemble)
 
     def send_degree(p):
         return remote(degs.at[xy_index(p)], deg_in.at[p], deg_s.at[p], deg_r.at[p], (row, xy_index(p)))
 
     loop(1, NC, lambda p: send_degree(p).start())
 
-    def multiply(matrix, index, right, add):
-        def chunk(m):
-            rows = pl.ds(pl.multiple_of(m * 512, 512), 512)
-            term = jnp.dot(matrix[index, rows, :], right, preferred_element_type=F32)
-            acc[rows, :] = acc[rows, :] + term if add else term
-
-        loop(0, 4, chunk)
+    def multiply(left, right, add):
+        term = jnp.dot(left, right, preferred_element_type=F32)
+        acc[...] = acc[...] + term if add else term
 
     def pair_of(ref, i):
         return jnp.concatenate([ref[2 * i], ref[2 * i + 1]], axis=0)
 
+    for side in range(2):
+        near(side, 1).wait_recv()
+        to_sibling((z + NZ - (1 - 2 * side)) % NZ).start()
     to_sibling(z).wait_recv()
-    multiply(a_ref, z, pair_of(x_all, z), False)
-
-    def arrive(i):
-        d = near_first(i)
-        agz(d).wait_recv()
-        to_sibling((z + NZ - d) % NZ).start()
-
-    arrive(1)
+    multiply(a_ref[z], pair_of(x_all, z), False)
 
     def forward(i):
-        arrive(i + 1)
-        zp = (z + NZ - near_first(i)) % NZ
+        zp = (z + pick(i, (6, 2, 7, 1, 5, 3))) % NZ
         to_sibling(zp).wait_recv()
-        multiply(a_ref, zp, pair_of(x_all, zp), True)
-
-    loop(1, NZ - 1, forward)
-    z_last = (z + NZ - NZ // 2) % NZ
+        multiply(a_ref[zp], pair_of(x_all, zp), True)
+
+    loop(0, 4, forward)
+    for side in range(2):
+        passed(side).wait_recv()
+        to_sibling((z + NZ - 3 * (1 - 2 * side)) % NZ).start()
+    z_last = (z + NZ // 2) % NZ
+    for side in range(2):
+        block = x_all.at[z_last * 2 + k, pl.ds(side * HALF, HALF)]
+        remote(block, block, agz_s.at[6 + side], agz_r.at[6 + side], sibling).wait_recv()
+    to_sibling(z_last).start()
+    loop(4, 6, forward)
     to_sibling(z_last).wait_recv()
 
-    def send_part(p):
-        return remote(part.at[xy_index(p)], part_in.at[p], rs_s.at[p], rs_r.at[p], (row, xy_index(p)))
+    def send_part(du, dv, relay, slot, sem):
+        return remote(part.at[at(du, dv)], part_in.at[slot], rs_s.at[sem], rs_r.at[slot], (row, at(*relay)))
+
+    def took_part(slot):
+        return remote(part_in.at[slot], part_in.at[slot], rs_s.at[0], rs_r.at[slot], sibling).wait_recv()
 
     x_last = pair_of(x_all, z_last)
 
-    def finish(p):
-        c = xy_index(p)
+    def finish(c):
         rows = pl.ds(pl.multiple_of(c * T, T), T)
         return acc[rows, :] + jnp.dot(a_ref[z_last, rows, :], x_last, preferred_element_type=F32)
 
+    def part_copy(i):
+        du, dv, ru, rv, slot = (pick(i, values) for values in zip(*FIRST_LEG))
+        return du, dv, send_part(du, dv, (ru, rv), slot, i)
+
     def finish_send(i):
-        p = (i + 9) % (NC - 1) + 1
-        part[xy_index(p)] = finish(p).astype(BF16)
-        send_part(p).start()
-
-    loop(0, NC - 1, finish_send)
-    own_sum[...] = finish(0)
-
-    def turn(q):
-        for e in range(2):
-            rows = pl.ds(pl.multiple_of((2 * q + e) * T, T), T)
-            for r in range(NR):
-                at_ref[q, r * T : (r + 1) * T, e * T : (e + 1) * T] = a_ref[
-                    r // 2, rows, (r % 2) * T : (r % 2 + 1) * T
-                ].T
+        du, dv, copy = part_copy(i)
+        part[at(du, dv)] = finish(at(du, dv)).astype(BF16)
+        copy.start()
+
+    loop(0, len(FIRST_LEG), finish_send)
+
+    def finish_line(j):
+        du, dv = (pick(j - 1, values) for values in zip(*LINES))
+        own_rows = pl.ds(pl.multiple_of(at(du, dv) * T, T), T)
+        acc[own_rows, :] = finish(at(du, dv))
+
+    loop(1, 4, finish_line)
+    own_sum[...] = finish(col)
+
+    def turn(c):
+        rows = pl.ds(pl.multiple_of(c * T, T), T)
+        for r in range(NR):
+            at_ref[c, r * T : (r + 1) * T, :] = a_ref[r // 2, rows, (r % 2) * T : (r % 2 + 1) * T].T
 
     loop(0, NC // 2, turn)
+
+    def send_line(j):
+        du, dv = (pick(j - 1, values) for values in zip(*LINES))
+        slot = pick(j - 1, (2, 3, 1))
+        return remote(line_sum.at[j], line_in.at[slot], rl_s.at[j], rl_r.at[slot], (row, at(du, dv)))
+
+    def add_line(j):
+        du, dv = (pick(j - 1, values) for values in zip(*LINES))
+        rows = pl.ds(pl.multiple_of(at(du, dv) * T, T), T)
+        total = acc[rows, :]
+        for e in range(1, 4):
+            took_part(4 * j + e)
+            total = total + part_in[4 * j + e].astype(F32)
+        line_sum[j] = total.astype(BF16)
+        send_line(j).start()
+
+    loop(1, 4, add_line)
+    loop(NC // 2, NC, turn)
     pre_self[...] = jnp.dot(feats[...], w_self[...], preferred_element_type=F32) + bias[...]
 
     own_degree = degs[col]
@@ -196,12 +281,12 @@
     scale = jnp.broadcast_to(scale_row, (T, T)).T
     scale = jnp.concatenate([scale, scale], axis=1)
 
-    def take_part(i):
-        p = (i + 9) % (NC - 1) + 1
-        send_part(p).wait_recv()
-        own_sum[...] = own_sum[...] + part_in[p].astype(F32)
-
-    loop(0, NC - 1, take_part)
+    for e in range(1, 4):
+        took_part(e)
+        own_sum[...] = own_sum[...] + part_in[e].astype(F32)
+    for e in range(1, 4):
+        remote(line_in.at[e], line_in.at[e], rl_s.at[0], rl_r.at[e], sibling).wait_recv()
+        own_sum[...] = own_sum[...] + line_in[e].astype(F32)
 
     mixed = (own_sum[...] * scale).astype(BF16)
     pre = pre_self[...] + jnp.dot(mixed, w_neigh[...], preferred_element_type=F32)
@@ -211,10 +296,22 @@
     back = lax.dot_general(grad_pre, w_neigh[...], NT, preferred_element_type=F32) * scale
     back_all[col] = back.astype(BF16)
 
-    def send_back(p):
-        return remote(back_all.at[col], back_all.at[col], ag_s.at[p], ag_r.at[p], (row, xy_index(p)))
-
-    loop(0, NC - 1, lambda i: send_back((i + 9) % (NC - 1) + 1).start())
+    def send_back(source, du, dv, sem):
+        return remote(back_all.at[source], back_all.at[source], ag_s.at[sem], ag_r.at[source], (row, at(du, dv)))
+
+    def own_back(i):
+        du, dv = (pick(i, values) for values in zip(*OWN_WAYS))
+        return send_back(col, du, dv, i)
+
+    def took_back(source):
+        remote(back_all.at[source], back_all.at[source], ag_s.at[0], ag_r.at[source], sibling).wait_recv()
+
+    def pass_back(f, e):
+        du, dv = LINES[f]
+        source = at(du, dv)
+        return send_back(source, *((0, e) if f == 0 else (e, 0)), 3 + 3 * f + 2 + e)
+
+    loop(0, len(OWN_WAYS), lambda i: own_back(i).start())
     out[...] = (pre * sig).astype(BF16)
 
     bias_sum = jnp.sum(grad_pre.astype(F32), axis=0, keepdims=True)
@@ -239,21 +336,26 @@
     loop(1, NZ, lambda d: send_w1(d).start())
     w1_in[z] = w1_out[z]
 
-    def await_pair(q):
-        yp = (y + q // 2) % NY
-        for e in range(2):
-            xp = ((x // 2 + q % 2) % 2) * 2 + e
-            send_back(((y + NY - yp) % NY) * NX + (x + NX - xp) % NX).wait_recv()
-        return yp * 2 + (x // 2 + q % 2) % 2
-
-    send_back((NX + x - (x + 1 - 2 * (x % 2))) % NX).wait_recv()
-    multiply(at_ref, col // 2, pair_of(back_all, col // 2), False)
-
-    def backward(q):
-        index = await_pair(q)
-        multiply(at_ref, index, pair_of(back_all, index), True)
-
-    loop(1, 6, backward)
+    for f in range(3):
+        took_back(at(*LINES[f]))
+        loop(1, 4, lambda e: pass_back(f, e).start())
+
+    def pair_at(i):
+        return tuple(at(*(pick(i, values) for values in zip(*(pair[n] for pair in PAIRS)))) for n in range(2))
+
+    def two_of(ref, a, b, axis):
+        return jnp.concatenate([ref[a], ref[b]], axis=axis)
+
+    a, b = pair_at(0)
+    multiply(two_of(at_ref, a, b, 1), two_of(back_all, a, b, 0), False)
+
+    def backward(i):
+        a, b = pair_at(i)
+        pl.when(i > 1)(lambda: took_back(a))
+        pl.when((i > 1))(lambda: took_back(b))
+        multiply(two_of(at_ref, a, b, 1), two_of(back_all, a, b, 0), True)
+
+    loop(1, 5, backward)
 
     def send_w2(p):
         return remote(w2_in.at[col], w2_in.at[col], w2_s.at[p], w2_r.at[p], (row, xy_index(p)))
@@ -265,43 +367,71 @@
     w2_in[col] = w1_sum.astype(BF16)
     loop(1, NC, lambda p: send_w2(p).start())
 
-    backward(6)
-    b_index = await_pair(7)
-    b_last = pair_of(back_all, b_index)
+    loop(5, 7, backward)
+    b_first, b_second = pair_at(7)
+    took_back(b_first)
+    took_back(b_second)
+    b_last = two_of(back_all, b_first, b_second, 0)
 
     def finish_back(r):
         rows = pl.ds(pl.multiple_of(r * T, T), T)
-        return acc[rows, :] + jnp.dot(at_ref[b_index, rows, :], b_last, preferred_element_type=F32)
-
-    def far_first(i):
-        return near_first(NZ - 1 - i)
+        left = jnp.concatenate([at_ref[b_first, rows, :], at_ref[b_second, rows, :]], axis=1)
+        return acc[rows, :] + jnp.dot(left, b_last, preferred_element_type=F32)
 
     def to_sibling_back(zp):
         return remote(sib_out.at[zp], sib_in.at[zp], bs_s.at[zp], bs_r.at[zp], sibling)
 
     def give_sibling(i):
-        zp = (z + far_first(i)) % NZ
+        zp = (z + pick(i, Z_ORDER)) % NZ
         sib_out[zp] = finish_back(zp * 2 + 1 - k).astype(BF16)
         to_sibling_back(zp).start()
 
     loop(0, NZ, give_sibling)
-
-    def send_comb(d):
-        zp = (z + d) % NZ
-        return remote(comb.at[zp], comb_in.at[d], rz_s.at[d], rz_r.at[d], z_to(d))
 
     def combine(zp):
         to_sibling_back(zp).wait_recv()
         return finish_back(zp * 2 + k) + sib_in[zp].astype(F32)
 
-    def combine_send(i):
-        d = far_first(i)
-        zp = (z + d) % NZ
+    def send_half(side):
+        sign = 1 - 2 * side
+        half = comb.at[(z + NZ // 2) % NZ, pl.ds(side * HALF, HALF)]
+        return remote(half, half_in.at[side], rz_s.at[side], rz_r.at[side], z_to(NZ - 2 * sign))
+
+    def send_far(side):
+        sign = 1 - 2 * side
+        block = comb.at[(z + NZ - 3 * sign) % NZ]
+        return remote(block, far_in.at[side], rz_s.at[2 + side], rz_r.at[2 + side], z_to(NZ - sign))
+
+    def send_comb(side, hops):
+        sign = 1 - 2 * side
+        slot = 2 * (hops - 1) + side
+        block = comb.at[(z + NZ - hops * sign) % NZ]
+        return remote(block, comb_in.at[slot], rz_s.at[4 + slot], rz_r.at[4 + slot], z_to(NZ - hops * sign))
+
+    z_four = (z + NZ // 2) % NZ
+    comb[z_four] = combine(z_four).astype(BF16)
+    for side in range(2):
+        send_half(side).start()
+    for side in range(2):
+        zp = (z + NZ - 3 * (1 - 2 * side)) % NZ
         comb[zp] = combine(zp).astype(BF16)
-        send_comb(d).start()
-
-    loop(0, NZ - 1, combine_send)
+        send_far(side).start()
+    for side in range(2):
+        zp = (z + NZ - (1 - 2 * side)) % NZ
+        comb[zp] = combine(zp).astype(BF16)
+        send_comb(side, 1).start()
     own_sum[...] = combine(z) + self_grad[...]
+    for side in range(2):
+        zp = (z + NZ - 2 * (1 - 2 * side)) % NZ
+        total = combine(zp)
+        send_far(side).wait_recv()
+        total = total + far_in[side].astype(F32)
+        send_half(side).wait_recv()
+        added = half_in[side].astype(F32)
+        zeros = jnp.zeros((HALF, F), F32)
+        total = total + jnp.concatenate([zeros, added] if side else [added, zeros], axis=0)
+        comb[zp] = total.astype(BF16)
+        send_comb(side, 2).start()
 
     loop(1, NC, lambda p: send_w2(p).wait_recv())
     w2_sum = w2_in[0].astype(F32)
@@ -315,12 +445,10 @@
 
     loop(1, NZ, lambda d: send_w3(d).start())
 
-    def take_comb(i):
-        d = far_first(i)
-        send_comb(d).wait_recv()
-        own_sum[...] = own_sum[...] + comb_in[d].astype(F32)
-
-    loop(0, NZ - 1, take_comb)
+    for hops in (1, 2):
+        for side in range(2):
+            send_comb(side, hops).wait_recv()
+            own_sum[...] = own_sum[...] + comb_in[2 * (hops - 1) + side].astype(F32)
     d_feats[...] = own_sum[...].astype(BF16)
 
     loop(1, NZ, lambda d: send_w3(d).wait_recv())
@@ -328,26 +456,37 @@
     w4.start()
     w4.wait_recv()
     core = jnp.full((F, F), k, jnp.int32)
-    mine = w3[...].reshape(F, F).astype(F32)
-    other = w3_in[...].reshape(F, F).astype(F32)
+    mine = w3[...].reshape(F, F)
+    other = w3_in[...].reshape(F, F)
     d_wself[...] = jnp.where(core == 0, mine, other)
     d_wneigh[...] = jnp.where(core == 0, other, mine)
 
+    for side in range(2):
+        near(side, 1).wait_send()
+        near(side, 2).wait_send()
+        passed(side).wait_send()
+        passed_half(side).wait_send()
+        send_half(side).wait_send()
+        send_far(side).wait_send()
+        send_comb(side, 1).wait_send()
+        send_comb(side, 2).wait_send()
+
     def sent_z(d):
-        agz(d).wait_send()
         send_w1(d).wait_send()
-        send_comb(d).wait_send()
         send_w3(d).wait_send()
 
     loop(1, NZ, sent_z)
 
     def sent_xy(p):
         send_degree(p).wait_send()
-        send_part(p).wait_send()
-        send_back(p).wait_send()
         send_w2(p).wait_send()
 
     loop(1, NC, sent_xy)
+    loop(0, len(FIRST_LEG), lambda i: part_copy(i)[2].wait_send())
+    loop(1, 4, lambda j: send_line(j).wait_send())
+    loop(0, len(OWN_WAYS), lambda i: own_back(i).wait_send())
+    for f in range(3):
+        loop(1, 4, lambda e: pass_back(f, e).wait_send())
 
     def sent_sibling(zp):
         to_sibling(zp).wait_send()
@@ -356,6 +495,11 @@
     loop(0, NZ, sent_sibling)
     w0.wait_send()
     w4.wait_send()
+
+
+def hand_over(*refs):
+    for source, target in zip(refs[:5], refs[5:]):
+        target[...] = source[...].astype(target.dtype)
 
 
 def per_device(feats, tiles, tile_row, tile_col, counts, w_self, w_neigh, bias, grad_out):
@@ -366,8 +510,8 @@
         out_shape=(
             jax.ShapeDtypeStruct((T, F), BF16),
             jax.ShapeDtypeStruct((T, F), BF16),
-            jax.ShapeDtypeStruct((F, F), F32),
-            jax.ShapeDtypeStruct((F, F), F32),
+            jax.ShapeDtypeStruct((F, F), BF16),
+            jax.ShapeDtypeStruct((F, F), BF16),
             jax.ShapeDtypeStruct((1, F), F32),
         ),
         in_specs=[
@@ -388,11 +532,13 @@
             pltpu.VMEM((8, F), jnp.int32),
             pltpu.SMEM((8, F), jnp.int32),
             pltpu.VMEM((NZ, NC * T, 2 * T), BF16),
-            pltpu.VMEM((NC // 2, NR * T, 2 * T), BF16),
+            pltpu.VMEM((NC, NR * T, T), BF16),
             pltpu.VMEM((NC * T, F), F32),
             pltpu.VMEM((NR, T, F), BF16),
             pltpu.VMEM((NC, T, F), BF16),
             pltpu.VMEM((NC, T, F), BF16),
+            pltpu.VMEM((4, T, F), BF16),
+            pltpu.VMEM((4, T, F), BF16),
             pltpu.VMEM((NC, 8, T), F32),
             pltpu.VMEM((NC, 8, T), F32),
             pltpu.VMEM((T, F), F32),
@@ -401,7 +547,9 @@
             pltpu.VMEM((NZ, T, F), BF16),
             pltpu.VMEM((NZ, T, F), BF16),
             pltpu.VMEM((NZ, T, F), BF16),
-            pltpu.VMEM((NZ, T, F), BF16),
+            pltpu.VMEM((2, T, F), BF16),
+            pltpu.VMEM((2, HALF, F), BF16),
+            pltpu.VMEM((4, T, F), BF16),
             pltpu.VMEM((2, F + 8, F), F32),
             pltpu.VMEM((F + 8, F), F32),
             pltpu.VMEM((NZ, WPART, F), BF16),
@@ -414,7 +562,9 @@
             dma,
         ]
         + [dma((NZ,))] * 4
-        + [dma((NC,))] * 6
+        + [dma((NC,))] * 4
+        + [dma((4,))] * 2
+        + [dma((NC,))] * 2
         + [dma((NZ,))] * 4
         + [dma, dma]
         + [dma((NZ,))] * 2
@@ -436,6 +586,13 @@
         bias.reshape(1, F),
         grad_out,
     )
+    outs = pl.pallas_call(
+        hand_over,
+        out_shape=[jax.ShapeDtypeStruct(o.shape, t) for o, t in zip(outs, (BF16, BF16, F32, F32, F32))],
+        in_specs=[vmem] * 5,
+        out_specs=[vmem] * 5,
+        name="hand_over",
+    )(*outs)
     return (outs[0], outs[1], outs[2], outs[3], outs[4].reshape(F))
 
 

time: 95.7 us -> 72.5 us (0.76)
  Pallas kernels: 86.6 us -> 71.1 us
  local copies, waits for them, and re-layouts: 7.5 us -> 0 us
    pallas_call x1, Pallas kernels: 86.6 us -> 69.2 us  [per_device(): pl.pallas_call(layer_kernel, out_shape=(jax.ShapeDtypeStruct((T, F), BF16...]
    unnamed x5 -> x0, local copies, waits for them, and re-layouts: 7.5 us -> none
    pallas_call x0 -> x1, Pallas kernels: none -> 1.88 us  [per_device(): pl.pallas_call(hand_over, out_shape=[jax.ShapeDtypeStruct(o.shape, t) for...]
where the time goes in v2:
time: 72.5 us; the launch traced here: 72.4 us
  Pallas kernels  71.1 us (98%)
  between operations  1.29 us (2%)
    pallas_call x1, Pallas kernels, per_device(): pl.pallas_call(layer_kernel, out_shape=(jax.ShapeDtypeStruct((T, F), BF16...  69.2 us
    pallas_call x1, Pallas kernels, per_device(): pl.pallas_call(hand_over, out_shape=[jax.ShapeDtypeStruct(o.shape, t) for...  1.88 us

profile of v2, /device:TPU:1, one launch (start us, length us, event | category | flops | bytes accessed | tf_op | source)
XLA Modules:
  0.0 72.4 jit_solution(8263302270727581121)
XLA Ops:
  1.3 69.2 %sage_layer.1 = (bf16[128,256]{1,0:T(8,128)(2,1)}, bf16[128,256]{1,0:T(8,128)(2,1)}, bf16[256,256]{1,0:T(8,128)(2,1)}, bf16[256,256]{1,0:T(8,128)(2,1)}, f32[1,256]{1,0:T(1,128)}) custom-call(bf16[128,256]{1,0:T(8,128)(2,1)} %feats.1, bf16[192,128,128]{2,1,0:T(8,128)(2,1)} %bitcast.3, s32[1,192]{1,0:T(1,128)} %tile_row.1, s32[1,192]{1,0:T(1,128)} %tile_col.1, ...), custom_call_target="tpu_custom_call" | custom-call | tf_op jit(solution)/shard_map/sage_layer/pallas_call | solution.py:508
  70.5 1.9 %hand_over.1 = (bf16[128,256]{1,0:T(8,128)(2,1)}, bf16[128,256]{1,0:T(8,128)(2,1)}, f32[256,256]{1,0:T(8,128)}, f32[256,256]{1,0:T(8,128)}, f32[1,256]{1,0:T(1,128)}) custom-call(bf16[128,256]{1,0:T(8,128)(2,1)} %get-tuple-element.15.refs_0_, bf16[128,256]{1,0:T(8,128)(2,1)} %get-tuple-element.16.refs_1_, bf16[256,256]{1,0:T(8,128)(2,1)} %get-tuple-element.17.refs_2_, ...), custom_call_target="tpu_custom_call" | custom-call | tf_op jit(solution)/shard_map/hand_over/pallas_call | solution.py:589

commit v3 on v2

--- a/solution.py
+++ b/solution.py
@@ -16,35 +16,39 @@
 SLOTS = 192
 TILE_CUTS = 6
 CUT = SLOTS // TILE_CUTS
-PART = F // NZ
+PART = F // NC
 HALF = T // 2
 WPART = PART + 16
 NT = (((1,), (1,)), ((), ()))
 TN = (((0,), (0,)), ((), ()))
 
 
-def first_legs():
-    legs = []
-    for du, dv in ((2, 2), (1, 1), (3, 3), (2, 1), (1, 2), (3, 1), (1, 3), (2, 3), (3, 2), (0, 2), (1, 0), (3, 0)):
-        if (du + dv) % 2 == 0:
-            relay, along, across = (0, dv), dv, du
-        else:
-            relay, along, across = (du, 0), du, dv
-        line = across // 2 if across % 2 == 0 else 2 + across // 2
-        legs.append((du, dv, *relay, line * 4 + (4 - along) % 4))
-    return tuple(legs)
-
-
-FIRST_LEG = first_legs()
-LINES = ((2, 0), (0, 1), (0, 3))
-OWN_WAYS = ((1, 0), (2, 0), (3, 0), (0, 1), (0, 2), (0, 3))
+FIRST_LEG = (
+    (2, 2, 0, 2, 1),
+    (2, 1, 0, 1, 4),
+    (2, 3, 0, 3, 3),
+    (1, 2, 1, 0, 2),
+    (3, 2, 3, 0, 0),
+    (1, 1, 1, 1, 5),
+    (1, 3, 1, 3, 6),
+    (3, 1, 3, 1, 7),
+    (3, 3, 3, 3, 8),
+    (1, 0, 1, 0, 9),
+    (3, 0, 3, 0, 10),
+    (0, 1, 0, 1, 11),
+    (0, 3, 0, 3, 12),
+)
+LINES = ((2, 0), (0, 2))
+LINE_SLOTS = ((0, 1, 2), (3, 4))
+OWN_WAYS = ((2, 0), (0, 2), (1, 0), (3, 0), (0, 1), (0, 3), (1, 1), (1, 3), (3, 1), (3, 3))
+PASSED = (((0, 2), (0, 1), (0, 3)), ((1, 0), (3, 0)))
 PAIRS = (
     ((0, 0), (2, 0)),
-    ((0, 1), (0, 3)),
-    ((1, 0), (3, 0)),
-    ((0, 2), (2, 2)),
-    ((1, 1), (3, 1)),
-    ((1, 3), (3, 3)),
+    ((0, 2), (1, 0)),
+    ((3, 0), (0, 1)),
+    ((0, 3), (1, 1)),
+    ((1, 3), (3, 1)),
+    ((3, 3), (2, 2)),
     ((2, 1), (2, 3)),
     ((1, 2), (3, 2)),
 )
@@ -52,6 +56,8 @@
 
 
 def pick(i, values):
+    if isinstance(i, int):
+        return values[i]
     chosen = values[0]
     for n, value in enumerate(values[1:], 1):
         chosen = jnp.where(i == n, value, chosen)
@@ -59,10 +65,10 @@
 
 
 def layer_kernel(
-    feats, tiles, tile_row, tile_col, counts, w_self, w_neigh, bias, grad_out,
+    feats, tiles, tile_row, tile_col, counts, w_self_h, w_neigh_h, bias, grad_out_h,
     out, d_feats, d_wself, d_wneigh, d_bias,
-    tiles_v, run, tab_v, tab, a_ref, at_ref, acc, x_all, part, part_in, line_sum, line_in, degs, deg_in, pre_self, own_sum,
-    back_all, sib_out, sib_in, comb, far_in, half_in, comb_in, grads, grads_in, w1_out, w1_in, w2_in, w3, w3_in, self_grad,
+    w_self, w_neigh, grad_out, late_sem, tiles_v, run, tab_v, tab, a_ref, at_ref, acc, x_all, part, part_in, line_sum, line_in, degs, deg_in, pre_self, own_sum,
+    back_all, sib_out, sib_in, comb, far_in, half_in, comb_in, grads, grads_in, w1_out, w1_in, w2_in, w3, w4_out, w4_in, self_grad,
     tile_sem, tab_sem, agz_s, agz_r, sib_s, sib_r, deg_s, deg_r, rs_s, rs_r, rl_s, rl_r, ag_s, ag_r, bs_s, bs_r, rz_s, rz_r,
     w0_s, w0_r, w1_s, w1_r, w2_s, w2_r, w3_s, w3_r, w4_s, w4_r,
 ):
@@ -102,6 +108,13 @@
 
     for i in range(TILE_CUTS):
         tile_copy(i).start()
+
+    late = [
+        pltpu.make_async_copy(source, target, late_sem.at[i])
+        for i, (source, target) in enumerate(((w_self_h, w_self), (w_neigh_h, w_neigh), (grad_out_h, grad_out)))
+    ]
+    for copy in late:
+        copy.start()
 
     barrier = pltpu.get_barrier_semaphore()
     pl.semaphore_signal(barrier, inc=1, device_id=sibling, device_id_type=MESH)
@@ -125,41 +138,55 @@
     tab_copy.start()
     x_all[row] = feats[...]
     run[SLOTS] = jnp.zeros((T, T), F32)
+
+    def add_up(s):
+        for e in range(4):
+            run[4 * s + e] = run[tab[0, 4 * s + e]] + tiles_v[4 * s + e].astype(F32)
+
+    def add_cut(i):
+        tile_copy(i).wait()
+        loop(i * CUT // 4, (i + 1) * CUT // 4, add_up)
+
+    tab_copy.wait()
+    for i in range(2):
+        add_cut(i)
     pl.semaphore_wait(barrier, 1 + (NZ - 1) + (NC - 1))
 
-    def near(side, hops):
+    def near(side):
+        return remote(feats, x_all.at[row], agz_s.at[2 + side], agz_r.at[2 + side], z_to(NZ + 1 - 2 * side))
+
+    def second(side, turn_in):
+        half = pl.ds(HALF * (side + turn_in - 2 * side * turn_in), HALF)
+        sem = 8 * turn_in + side
+        return remote(
+            feats.at[half], x_all.at[row, half], agz_s.at[sem], agz_r.at[sem], z_to(NZ + 2 * (1 - 2 * side))
+        )
+
+    def passed(side, turn_in):
         sign = 1 - 2 * side
-        return remote(
-            feats, x_all.at[row], agz_s.at[2 * hops + side - 2], agz_r.at[2 * hops + side - 2], z_to(NZ + sign * hops)
-        )
-
-    def passed(side):
-        sign = 1 - 2 * side
-        block = x_all.at[((z + NZ - 2 * sign) % NZ) * 2 + k]
-        return remote(block, block, agz_s.at[4 + side], agz_r.at[4 + side], z_to(NZ + sign))
+        half = pl.ds(HALF * (side + turn_in - 2 * side * turn_in), HALF)
+        block = x_all.at[((z + NZ - 2 * sign) % NZ) * 2 + k, half]
+        sem = 4 + 6 * turn_in + side
+        return remote(block, block, agz_s.at[sem], agz_r.at[sem], z_to(NZ + sign))
 
     def passed_half(side):
         sign = 1 - 2 * side
         block = x_all.at[((z + NZ - 2 * sign) % NZ) * 2 + k, pl.ds(side * HALF, HALF)]
         return remote(block, block, agz_s.at[6 + side], agz_r.at[6 + side], z_to(NZ + 2 * sign))
 
-    for hops in (2, 1):
+    for turn_in in range(2):
         for side in range(2):
-            near(side, hops).start()
+            second(side, turn_in).start()
+    for side in range(2):
+        near(side).start()
 
     def to_sibling(zp):
         return remote(x_all.at[zp * 2 + k], x_all.at[zp * 2 + k], sib_s.at[zp], sib_r.at[zp], sibling)
 
     to_sibling(z).start()
 
-    tab_copy.wait()
-    for i in range(TILE_CUTS):
-        tile_copy(i).wait()
-
-        def add_up(s):
-            run[s] = run[tab[0, s]] + tiles_v[s].astype(F32)
-
-        loop(i * CUT, (i + 1) * CUT, add_up)
+    for i in range(2, TILE_CUTS):
+        add_cut(i)
 
     def assemble(c):
         rows = pl.ds(pl.multiple_of(c * T, T), T)
@@ -174,15 +201,18 @@
 
     loop(0, NC // 2, assemble)
     for side in range(2):
-        sign = 1 - 2 * side
-        near(side, 2).wait_recv()
+        second(side, 0).wait_recv()
         passed_half(side).start()
-        passed(side).start()
-        to_sibling((z + NZ - 2 * sign) % NZ).start()
+        passed(side, 0).start()
+    for side in range(2):
+        second(side, 1).wait_recv()
+        passed(side, 1).start()
+        to_sibling((z + NZ - 2 * (1 - 2 * side)) % NZ).start()
     loop(NC // 2, NC, assemble)
 
     def send_degree(p):
         return remote(degs.at[xy_index(p)], deg_in.at[p], deg_s.at[p], deg_r.at[p], (row, xy_index(p)))
+
 
     loop(1, NC, lambda p: send_degree(p).start())
 
@@ -194,7 +224,7 @@
         return jnp.concatenate([ref[2 * i], ref[2 * i + 1]], axis=0)
 
     for side in range(2):
-        near(side, 1).wait_recv()
+        near(side).wait_recv()
         to_sibling((z + NZ - (1 - 2 * side)) % NZ).start()
     to_sibling(z).wait_recv()
     multiply(a_ref[z], pair_of(x_all, z), False)
@@ -206,7 +236,8 @@
 
     loop(0, 4, forward)
     for side in range(2):
-        passed(side).wait_recv()
+        passed(side, 0).wait_recv()
+        passed(side, 1).wait_recv()
         to_sibling((z + NZ - 3 * (1 - 2 * side)) % NZ).start()
     z_last = (z + NZ // 2) % NZ
     for side in range(2):
@@ -237,15 +268,18 @@
         part[at(du, dv)] = finish(at(du, dv)).astype(BF16)
         copy.start()
 
-    loop(0, len(FIRST_LEG), finish_send)
+    for i in range(len(FIRST_LEG)):
+        finish_send(i)
 
     def finish_line(j):
-        du, dv = (pick(j - 1, values) for values in zip(*LINES))
+        du, dv = LINES[j]
         own_rows = pl.ds(pl.multiple_of(at(du, dv) * T, T), T)
         acc[own_rows, :] = finish(at(du, dv))
 
-    loop(1, 4, finish_line)
+    for j in range(2):
+        finish_line(j)
     own_sum[...] = finish(col)
+
 
     def turn(c):
         rows = pl.ds(pl.multiple_of(c * T, T), T)
@@ -255,22 +289,22 @@
     loop(0, NC // 2, turn)
 
     def send_line(j):
-        du, dv = (pick(j - 1, values) for values in zip(*LINES))
-        slot = pick(j - 1, (2, 3, 1))
-        return remote(line_sum.at[j], line_in.at[slot], rl_s.at[j], rl_r.at[slot], (row, at(du, dv)))
+        return remote(line_sum.at[j], line_in.at[j], rl_s.at[j], rl_r.at[j], (row, at(*LINES[j])))
 
     def add_line(j):
-        du, dv = (pick(j - 1, values) for values in zip(*LINES))
-        rows = pl.ds(pl.multiple_of(at(du, dv) * T, T), T)
+        rows = pl.ds(pl.multiple_of(at(*LINES[j]) * T, T), T)
         total = acc[rows, :]
-        for e in range(1, 4):
-            took_part(4 * j + e)
-            total = total + part_in[4 * j + e].astype(F32)
+        for slot in LINE_SLOTS[j]:
+            took_part(slot)
+            total = total + part_in[slot].astype(F32)
         line_sum[j] = total.astype(BF16)
         send_line(j).start()
 
-    loop(1, 4, add_line)
+    for j in range(2):
+        add_line(j)
     loop(NC // 2, NC, turn)
+    for copy in late:
+        copy.wait()
     pre_self[...] = jnp.dot(feats[...], w_self[...], preferred_element_type=F32) + bias[...]
 
     own_degree = degs[col]
@@ -281,12 +315,14 @@
     scale = jnp.broadcast_to(scale_row, (T, T)).T
     scale = jnp.concatenate([scale, scale], axis=1)
 
-    for e in range(1, 4):
-        took_part(e)
-        own_sum[...] = own_sum[...] + part_in[e].astype(F32)
-    for e in range(1, 4):
-        remote(line_in.at[e], line_in.at[e], rl_s.at[0], rl_r.at[e], sibling).wait_recv()
-        own_sum[...] = own_sum[...] + line_in[e].astype(F32)
+    def add_direct(slot):
+        took_part(slot)
+        own_sum[...] = own_sum[...] + part_in[slot].astype(F32)
+
+    loop(5, 13, add_direct)
+    for j in range(2):
+        send_line(j).wait_recv()
+        own_sum[...] = own_sum[...] + line_in[j].astype(F32)
 
     mixed = (own_sum[...] * scale).astype(BF16)
     pre = pre_self[...] + jnp.dot(mixed, w_neigh[...], preferred_element_type=F32)
@@ -307,38 +343,39 @@
         remote(back_all.at[source], back_all.at[source], ag_s.at[0], ag_r.at[source], sibling).wait_recv()
 
     def pass_back(f, e):
-        du, dv = LINES[f]
-        source = at(du, dv)
-        return send_back(source, *((0, e) if f == 0 else (e, 0)), 3 + 3 * f + 2 + e)
-
-    loop(0, len(OWN_WAYS), lambda i: own_back(i).start())
+        return send_back(at(*LINES[f]), *PASSED[f][e], len(OWN_WAYS) + 3 * f + e)
+
+    for i in range(6):
+        own_back(i).start()
     out[...] = (pre * sig).astype(BF16)
 
     bias_sum = jnp.sum(grad_pre.astype(F32), axis=0, keepdims=True)
-    grads[0, 0:F, :] = lax.dot_general(feats[...], grad_pre, TN, preferred_element_type=F32)
-    grads[1, 0:F, :] = lax.dot_general(mixed, grad_pre, TN, preferred_element_type=F32)
-    grads[0, F : F + 8, :] = jnp.broadcast_to(bias_sum, (8, F))
-    grads[1, F : F + 8, :] = jnp.broadcast_to(bias_sum, (8, F))
+    grads[0, 0:F, :] = lax.dot_general(feats[...], grad_pre, TN, preferred_element_type=F32).astype(BF16)
+    grads[1, 0:F, :] = lax.dot_general(mixed, grad_pre, TN, preferred_element_type=F32).astype(BF16)
+    for i in range(2):
+        grads[i, F : F + PART, :] = jnp.broadcast_to(bias_sum, (PART, F)).astype(BF16)
     w0 = remote(grads.at[1 - k], grads_in, w0_s, w0_r, sibling)
     w0.start()
     self_grad[...] = lax.dot_general(grad_pre, w_self[...], NT, preferred_element_type=F32)
     w0.wait_recv()
-    bias_two = (grads[k, F : F + 8, :] + grads_in[F : F + 8, :])[0:1, :]
-
-    def send_w1(d):
-        zp = (z + d) % NZ
-        return remote(w1_out.at[zp], w1_in.at[z], w1_s.at[d], w1_r.at[d], z_to(d))
-
-    for zp in range(NZ):
-        rows = slice(zp * PART, (zp + 1) * PART)
-        w1_out[zp, 0:PART, :] = (grads[k, rows, :] + grads_in[rows, :]).astype(BF16)
-        w1_out[zp, PART:WPART, :] = jnp.broadcast_to(bias_two, (16, F)).astype(BF16)
-    loop(1, NZ, lambda d: send_w1(d).start())
-    w1_in[z] = w1_out[z]
-
-    for f in range(3):
+    bias_rows = slice(F, F + PART)
+    bias_two = grads[k, bias_rows, :].astype(F32) + grads_in[bias_rows, :].astype(F32)
+
+    def send_w1(p):
+        return remote(w1_out.at[xy_index(p)], w1_in.at[p], w1_s.at[p], w1_r.at[p], (row, xy_index(p)))
+
+    for c in range(NC):
+        rows = slice(c * PART, (c + 1) * PART)
+        w1_out[c] = (grads[k, rows, :].astype(F32) + grads_in[rows, :].astype(F32)).astype(BF16)
+    loop(1, NC, lambda p: send_w1(p).start())
+    for i in range(6, len(OWN_WAYS)):
+        own_back(i).start()
+    w2_in[z, PART:WPART, :] = bias_two.astype(BF16)
+
+    for f in range(2):
         took_back(at(*LINES[f]))
-        loop(1, 4, lambda e: pass_back(f, e).start())
+        for e in range(len(PASSED[f])):
+            pass_back(f, e).start()
 
     def pair_at(i):
         return tuple(at(*(pick(i, values) for values in zip(*(pair[n] for pair in PAIRS)))) for n in range(2))
@@ -352,22 +389,23 @@
     def backward(i):
         a, b = pair_at(i)
         pl.when(i > 1)(lambda: took_back(a))
-        pl.when((i > 1))(lambda: took_back(b))
+        took_back(b)
         multiply(two_of(at_ref, a, b, 1), two_of(back_all, a, b, 0), True)
 
-    loop(1, 5, backward)
-
-    def send_w2(p):
-        return remote(w2_in.at[col], w2_in.at[col], w2_s.at[p], w2_r.at[p], (row, xy_index(p)))
-
-    loop(1, NZ, lambda d: send_w1(d).wait_recv())
-    w1_sum = w1_in[0].astype(F32)
-    for zp in range(1, NZ):
-        w1_sum = w1_sum + w1_in[zp].astype(F32)
-    w2_in[col] = w1_sum.astype(BF16)
-    loop(1, NC, lambda p: send_w2(p).start())
-
-    loop(5, 7, backward)
+    loop(1, 3, backward)
+
+    loop(1, NC, lambda p: send_w1(p).wait_recv())
+    w1_sum = w1_out[col].astype(F32)
+    for p in range(1, NC):
+        w1_sum = w1_sum + w1_in[p].astype(F32)
+    w2_in[z, 0:PART, :] = w1_sum.astype(BF16)
+
+    def send_w2(d):
+        return remote(w2_in.at[z], w2_in.at[z], w2_s.at[d], w2_r.at[d], z_to(d))
+
+    loop(1, NZ, lambda d: send_w2(d).start())
+
+    loop(3, 7, backward)
     b_first, b_second = pair_at(7)
     took_back(b_first)
     took_back(b_second)
@@ -386,7 +424,8 @@
         sib_out[zp] = finish_back(zp * 2 + 1 - k).astype(BF16)
         to_sibling_back(zp).start()
 
-    loop(0, NZ, give_sibling)
+    for i in range(NZ):
+        give_sibling(i)
 
     def combine(zp):
         to_sibling_back(zp).wait_recv()
@@ -421,6 +460,18 @@
         comb[zp] = combine(zp).astype(BF16)
         send_comb(side, 1).start()
     own_sum[...] = combine(z) + self_grad[...]
+
+    loop(1, NZ, lambda d: send_w2(d).wait_recv())
+    w2_sum = w2_in[0].astype(F32)
+    for zp in range(1, NZ):
+        w2_sum = w2_sum + w2_in[zp].astype(F32)
+    w3[col] = w2_sum.astype(BF16)
+
+    def send_w3(p):
+        return remote(w3.at[col], w3.at[col], w3_s.at[p], w3_r.at[p], (row, xy_index(p)))
+
+    loop(1, NC, lambda p: send_w3(p).start())
+
     for side in range(2):
         zp = (z + NZ - 2 * (1 - 2 * side)) % NZ
         total = combine(zp)
@@ -433,17 +484,15 @@
         comb[zp] = total.astype(BF16)
         send_comb(side, 2).start()
 
-    loop(1, NC, lambda p: send_w2(p).wait_recv())
-    w2_sum = w2_in[0].astype(F32)
+    loop(1, NC, lambda p: send_w3(p).wait_recv())
+    bias_all = w3[0, PART : PART + 1, :].astype(F32)
     for c in range(1, NC):
-        w2_sum = w2_sum + w2_in[c].astype(F32)
-    d_bias[...] = w2_sum[PART : PART + 1, :]
-    w3[z] = w2_sum[0:PART, :].astype(BF16)
-
-    def send_w3(d):
-        return remote(w3.at[z], w3.at[z], w3_s.at[d], w3_r.at[d], z_to(d))
-
-    loop(1, NZ, lambda d: send_w3(d).start())
+        bias_all = bias_all + w3[c, PART : PART + 1, :].astype(F32)
+    d_bias[...] = bias_all
+    for c in range(NC):
+        w4_out[c * PART : (c + 1) * PART, :] = w3[c, 0:PART, :]
+    w4 = remote(w4_out, w4_in, w4_s, w4_r, sibling)
+    w4.start()
 
     for hops in (1, 2):
         for side in range(2):
@@ -451,20 +500,18 @@
             own_sum[...] = own_sum[...] + comb_in[2 * (hops - 1) + side].astype(F32)
     d_feats[...] = own_sum[...].astype(BF16)
 
-    loop(1, NZ, lambda d: send_w3(d).wait_recv())
-    w4 = remote(w3, w3_in, w4_s, w4_r, sibling)
-    w4.start()
     w4.wait_recv()
     core = jnp.full((F, F), k, jnp.int32)
-    mine = w3[...].reshape(F, F)
-    other = w3_in[...].reshape(F, F)
+    mine = w4_out[...]
+    other = w4_in[...]
     d_wself[...] = jnp.where(core == 0, mine, other)
     d_wneigh[...] = jnp.where(core == 0, other, mine)
 
     for side in range(2):
-        near(side, 1).wait_send()
-        near(side, 2).wait_send()
-        passed(side).wait_send()
+        near(side).wait_send()
+        for turn_in in range(2):
+            second(side, turn_in).wait_send()
+            passed(side, turn_in).wait_send()
         passed_half(side).wait_send()
         send_half(side).wait_send()
         send_far(side).wait_send()
@@ -472,21 +519,23 @@
         send_comb(side, 2).wait_send()
 
     def sent_z(d):
-        send_w1(d).wait_send()
-        send_w3(d).wait_send()
+        send_w2(d).wait_send()
 
     loop(1, NZ, sent_z)
 
     def sent_xy(p):
         send_degree(p).wait_send()
-        send_w2(p).wait_send()
+        send_w1(p).wait_send()
+        send_w3(p).wait_send()
 
     loop(1, NC, sent_xy)
     loop(0, len(FIRST_LEG), lambda i: part_copy(i)[2].wait_send())
-    loop(1, 4, lambda j: send_line(j).wait_send())
+    for j in range(2):
+        send_line(j).wait_send()
     loop(0, len(OWN_WAYS), lambda i: own_back(i).wait_send())
-    for f in range(3):
-        loop(1, 4, lambda e: pass_back(f, e).wait_send())
+    for f in range(2):
+        for e in range(len(PASSED[f])):
+            pass_back(f, e).wait_send()
 
     def sent_sibling(zp):
         to_sibling(zp).wait_send()
@@ -520,13 +569,17 @@
             vmem,
             vmem,
             pl.BlockSpec(memory_space=pltpu.SMEM),
+            pl.BlockSpec(memory_space=pl.ANY),
+            pl.BlockSpec(memory_space=pl.ANY),
             vmem,
-            vmem,
-            vmem,
-            vmem,
+            pl.BlockSpec(memory_space=pl.ANY),
         ],
         out_specs=(vmem,) * 5,
         scratch_shapes=[
+            pltpu.VMEM((F, F), BF16),
+            pltpu.VMEM((F, F), BF16),
+            pltpu.VMEM((T, F), BF16),
+            dma((3,)),
             pltpu.VMEM((SLOTS, T, T), BF16),
             pltpu.VMEM((SLOTS + 1, T, T), F32),
             pltpu.VMEM((8, F), jnp.int32),
@@ -537,8 +590,8 @@
             pltpu.VMEM((NR, T, F), BF16),
             pltpu.VMEM((NC, T, F), BF16),
             pltpu.VMEM((NC, T, F), BF16),
-            pltpu.VMEM((4, T, F), BF16),
-            pltpu.VMEM((4, T, F), BF16),
+            pltpu.VMEM((2, T, F), BF16),
+            pltpu.VMEM((2, T, F), BF16),
             pltpu.VMEM((NC, 8, T), F32),
             pltpu.VMEM((NC, 8, T), F32),
             pltpu.VMEM((T, F), F32),
@@ -550,26 +603,28 @@
             pltpu.VMEM((2, T, F), BF16),
             pltpu.VMEM((2, HALF, F), BF16),
             pltpu.VMEM((4, T, F), BF16),
-            pltpu.VMEM((2, F + 8, F), F32),
-            pltpu.VMEM((F + 8, F), F32),
-            pltpu.VMEM((NZ, WPART, F), BF16),
+            pltpu.VMEM((2, F + PART, F), BF16),
+            pltpu.VMEM((F + PART, F), BF16),
+            pltpu.VMEM((NC, PART, F), BF16),
+            pltpu.VMEM((NC, PART, F), BF16),
             pltpu.VMEM((NZ, WPART, F), BF16),
             pltpu.VMEM((NC, WPART, F), BF16),
-            pltpu.VMEM((NZ, PART, F), BF16),
-            pltpu.VMEM((NZ, PART, F), BF16),
+            pltpu.VMEM((F, F), BF16),
+            pltpu.VMEM((F, F), BF16),
             pltpu.VMEM((T, F), F32),
             dma((TILE_CUTS,)),
             dma,
         ]
-        + [dma((NZ,))] * 4
+        + [dma((NZ + 4,))] * 2
+        + [dma((NZ,))] * 2
         + [dma((NC,))] * 4
-        + [dma((4,))] * 2
+        + [dma((2,))] * 2
         + [dma((NC,))] * 2
         + [dma((NZ,))] * 4
         + [dma, dma]
+        + [dma((NC,))] * 2
         + [dma((NZ,))] * 2
         + [dma((NC,))] * 2
-        + [dma((NZ,))] * 2
         + [dma, dma],
         compiler_params=pltpu.CompilerParams(
             collective_id=0, has_side_effects=True, vmem_limit_bytes=56 * 2**20

time: 72.5 us -> 66.8 us (0.921)
  Pallas kernels: 71.1 us -> 65.3 us
    pallas_call x1, Pallas kernels: 69.2 us -> 63.5 us  [per_device(): pl.pallas_call(layer_kernel, out_shape=(jax.ShapeDtypeStruct((T, F), BF16...]
where the time goes in v3:
time: 66.8 us; the launch traced here: 66.6 us
  Pallas kernels  65.3 us (98%)
  between operations  1.29 us (2%)
    pallas_call x1, Pallas kernels, per_device(): pl.pallas_call(layer_kernel, out_shape=(jax.ShapeDtypeStruct((T, F), BF16...  63.5 us
    pallas_call x1, Pallas kernels, per_device(): pl.pallas_call(hand_over, out_shape=[jax.ShapeDtypeStruct(o.shape, t) for...  1.88 us

profile of v3, /device:TPU:1, one launch (start us, length us, event | category | flops | bytes accessed | tf_op | source)
XLA Modules:
  0.0 66.6 jit_solution(8086291798801531935)
XLA Ops:
  1.3 63.5 %sage_layer.1 = (bf16[128,256]{1,0:T(8,128)(2,1)}, bf16[128,256]{1,0:T(8,128)(2,1)}, bf16[256,256]{1,0:T(8,128)(2,1)}, bf16[256,256]{1,0:T(8,128)(2,1)}, f32[1,256]{1,0:T(1,128)}) custom-call(bf16[128,256]{1,0:T(8,128)(2,1)} %feats.1, bf16[192,128,128]{2,1,0:T(8,128)(2,1)} %bitcast.3, s32[1,192]{1,0:T(1,128)} %tile_row.1, s32[1,192]{1,0:T(1,128)} %tile_col.1, ...), custom_call_target="tpu_custom_call" | custom-call | tf_op jit(solution)/shard_map/sage_layer/pallas_call | solution.py:557
  64.7 1.9 %hand_over.1 = (bf16[128,256]{1,0:T(8,128)(2,1)}, bf16[128,256]{1,0:T(8,128)(2,1)}, f32[256,256]{1,0:T(8,128)}, f32[256,256]{1,0:T(8,128)}, f32[1,256]{1,0:T(1,128)}) custom-call(bf16[128,256]{1,0:T(8,128)(2,1)} %get-tuple-element.15.refs_0_, bf16[128,256]{1,0:T(8,128)(2,1)} %get-tuple-element.16.refs_1_, bf16[256,256]{1,0:T(8,128)(2,1)} %get-tuple-element.17.refs_2_, ...), custom_call_target="tpu_custom_call" | custom-call | tf_op jit(solution)/shard_map/hand_over/pallas_call | solution.py:644

commit v4 on v3

--- a/solution.py
+++ b/solution.py
@@ -367,7 +367,8 @@
     for c in range(NC):
         rows = slice(c * PART, (c + 1) * PART)
         w1_out[c] = (grads[k, rows, :].astype(F32) + grads_in[rows, :].astype(F32)).astype(BF16)
-    loop(1, NC, lambda p: send_w1(p).start())
+    for p in range(1, NC):
+        send_w1(p).start()
     for i in range(6, len(OWN_WAYS)):
         own_back(i).start()
     w2_in[z, PART:WPART, :] = bias_two.astype(BF16)
@@ -403,7 +404,8 @@
     def send_w2(d):
         return remote(w2_in.at[z], w2_in.at[z], w2_s.at[d], w2_r.at[d], z_to(d))
 
-    loop(1, NZ, lambda d: send_w2(d).start())
+    for d in range(1, NZ):
+        send_w2(d).start()
 
     loop(3, 7, backward)
     b_first, b_second = pair_at(7)
@@ -470,7 +472,8 @@
     def send_w3(p):
         return remote(w3.at[col], w3.at[col], w3_s.at[p], w3_r.at[p], (row, xy_index(p)))
 
-    loop(1, NC, lambda p: send_w3(p).start())
+    for p in range(1, NC):
+        send_w3(p).start()
 
     for side in range(2):
         zp = (z + NZ - 2 * (1 - 2 * side)) % NZ

time: 66.8 us -> 66.8 us (level)
  no operation moved by 1% of the time
where the time goes in v4:
time: 66.8 us; the launch traced here: 66.6 us
  Pallas kernels  65.3 us (98%)
  between operations  1.29 us (2%)
    pallas_call x1, Pallas kernels, per_device(): pl.pallas_call(layer_kernel, out_shape=(jax.ShapeDtypeStruct((T, F), BF16...  63.4 us
    pallas_call x1, Pallas kernels, per_device(): pl.pallas_call(hand_over, out_shape=[jax.ShapeDtypeStruct(o.shape, t) for...  1.88 us

profile of v4, /device:TPU:1, one launch (start us, length us, event | category | flops | bytes accessed | tf_op | source)
XLA Modules:
  0.0 66.6 jit_solution(715189110934565805)
XLA Ops:
  1.3 63.4 %sage_layer.1 = (bf16[128,256]{1,0:T(8,128)(2,1)}, bf16[128,256]{1,0:T(8,128)(2,1)}, bf16[256,256]{1,0:T(8,128)(2,1)}, bf16[256,256]{1,0:T(8,128)(2,1)}, f32[1,256]{1,0:T(1,128)}) custom-call(bf16[128,256]{1,0:T(8,128)(2,1)} %feats.1, bf16[192,128,128]{2,1,0:T(8,128)(2,1)} %bitcast.3, s32[1,192]{1,0:T(1,128)} %tile_row.1, s32[1,192]{1,0:T(1,128)} %tile_col.1, ...), custom_call_target="tpu_custom_call" | custom-call | tf_op jit(solution)/shard_map/sage_layer/pallas_call | solution.py:560
  64.7 1.9 %hand_over.1 = (bf16[128,256]{1,0:T(8,128)(2,1)}, bf16[128,256]{1,0:T(8,128)(2,1)}, f32[256,256]{1,0:T(8,128)}, f32[256,256]{1,0:T(8,128)}, f32[1,256]{1,0:T(1,128)}) custom-call(bf16[128,256]{1,0:T(8,128)(2,1)} %get-tuple-element.15.refs_0_, bf16[128,256]{1,0:T(8,128)(2,1)} %get-tuple-element.16.refs_1_, bf16[256,256]{1,0:T(8,128)(2,1)} %get-tuple-element.17.refs_2_, ...), custom_call_target="tpu_custom_call" | custom-call | tf_op jit(solution)/shard_map/hand_over/pallas_call | solution.py:647
